TPU v7x, 256 devices: a whole 4x4x8 slice. The times are simulated.
256 devices in a mesh: seq: 32 (over y, z), chan: 8 (over x, core).
Axes of the slice: x: 4, y: 4, z: 8, core: 2. Of those that a mesh axis runs over, the one named last changes fastest.
Arguments:
- query_mr: bfloat16 [4096, 8192], P('seq', 'chan'), may hold values from -6 to 6
- key_mr: bfloat16 [4096, 8192], P('seq', 'chan'), may hold values from -6 to 6
- value_mr: bfloat16 [4096, 8192], P('seq', 'chan'), may hold values from -6 to 6
- query_li: bfloat16 [4096, 8192], P('seq', 'chan'), may hold values from -6 to 6
- key_li: bfloat16 [4096, 8192], P('seq', 'chan'), may hold values from -6 to 6
- cotangent: bfloat16 [4096, 8192], P('seq', 'chan'), may hold values from -40 to 40
- mr_filter: float32 [512, 128], P('chan'), may hold values from -3.535534 to 3.535534
- norm_gain: float32 [8192], P('chan'), may hold values from 0.1 to 1.9
- li_decay: float32 [512, 16], P('chan'), may hold values from 0.00012207031 to 0.03
- li_residue: float32 [512, 16], P('chan'), may hold values from -1 to 1
Outputs:
- out_li: bfloat16 [4096, 8192], P('seq', 'chan')
- grad_query_mr: bfloat16 [4096, 8192], P('seq', 'chan')
- grad_key_mr: bfloat16 [4096, 8192], P('seq', 'chan')
- grad_value_mr: bfloat16 [4096, 8192], P('seq', 'chan')
- grad_query_li: bfloat16 [4096, 8192], P('seq', 'chan')
- grad_key_li: bfloat16 [4096, 8192], P('seq', 'chan')
- grad_gain: float32 [8192], P('chan')
- grad_filter: float32 [512, 128], P('chan')
All inputs are finite; a program needn't handle non-finite values.
Results may differ from a plain program's by a relative error of at most 0.025.
Values may be sent and summed in bfloat16 or wider, within the bound.
A program may use at most 128 MiB of HBM per device.

v0:
```python
import jax
import jax.numpy as jnp
from jax import lax
from jax.sharding import PartitionSpec as P

D = 8192
G = 512
LBLK = 128


HIGHEST = lax.Precision.HIGHEST


def from_behind(value, axis, steps):
    count = lax.axis_size(axis)
    initial, last = (max(0, -steps), min(count, count - steps))
    return lax.ppermute(value, axis, [(source, source + steps) for source in range(initial, last)])


def toeplitz(edge_row):
    group_count, double_len = edge_row.shape
    block_len = double_len // 2
    cyclic = jnp.roll(jnp.flip(edge_row, -1), block_len + 1, axis=-1)
    repeated = jnp.tile(cyclic, (1, block_len))
    shaped = repeated[:, : block_len * (double_len - 1)].reshape(
        group_count, block_len, double_len - 1
    )
    return shaped[:, :, :block_len]


def combine_pair(earlier, latter):
    return (earlier[0] * latter[0], latter[1] + latter[0][..., None] * earlier[1])


def modal_parts(blocks, decays, residues, backward):
    block_len = blocks.shape[1]
    offsets = jnp.arange(block_len, dtype=jnp.float32)
    rate_col = decays[:, :, None]
    weights_res = residues * jnp.sqrt(2.0 * decays)
    fading = jnp.exp(-rate_col * offsets)
    filter_taps = jnp.einsum("gr,grd->gd", weights_res, fading, precision=HIGHEST)
    matrix = toeplitz(jnp.concatenate([jnp.zeros_like(filter_taps), filter_taps], -1))
    if backward:
        inside = jnp.einsum("gji,bjgc->bigc", matrix, blocks, precision=HIGHEST)
        weigh_in = fading
        weigh_out = weights_res[:, :, None] * jnp.exp(-rate_col * (block_len - offsets))
    else:
        inside = jnp.einsum("gij,bjgc->bigc", matrix, blocks, precision=HIGHEST)
        weigh_in = jnp.exp(-rate_col * (block_len - 1.0 - offsets))
        weigh_out = weights_res[:, :, None] * jnp.exp(-rate_col * (offsets + 1.0))
    states = jnp.einsum("grj,bjgc->bgrc", weigh_in, blocks, precision=HIGHEST)
    powers = jnp.broadcast_to(jnp.exp(-decays * block_len), (blocks.shape[0],) + decays.shape)
    running = lax.associative_scan(combine_pair, (powers, states), reverse=backward, axis=0)
    return (inside, weigh_out, running)


def modal_finish(inside, weigh_out, running, incoming, backward):
    powers, states = running
    if backward:
        prior_pow = jnp.concatenate([powers[1:], jnp.ones_like(powers[:1])], 0)
        prior_sum = jnp.concatenate([states[1:], jnp.zeros_like(states[:1])], 0)
    else:
        prior_pow = jnp.concatenate([jnp.ones_like(powers[:1]), powers[:-1]], 0)
        prior_sum = jnp.concatenate([jnp.zeros_like(states[:1]), states[:-1]], 0)
    entering = prior_sum + prior_pow[..., None] * incoming[None]
    return inside + jnp.einsum("gri,bgrc->bigc", weigh_out, entering, precision=HIGHEST)


def local_long(columns, decays, residues, backward):
    seq_len, chan_count = columns.shape
    group_size = D // G
    blocks = columns.reshape(seq_len // LBLK, LBLK, chan_count // group_size, group_size)
    inside, weigh_out, running = modal_parts(blocks, decays, residues, backward)
    incoming = jnp.zeros_like(running[1][0])
    return modal_finish(inside, weigh_out, running, incoming, backward).reshape(seq_len, chan_count)


def on_device(
    query_mr,
    key_mr,
    value_mr,
    query_li,
    key_li,
    cotangent,
    mr_filter,
    norm_gain,
    li_decay,
    li_residue,
):
    row_count, chan_count = query_mr.shape
    group_count, tap_count = mr_filter.shape
    group_size = chan_count // group_count
    block_count = row_count // tap_count
    grad_scale = float(row_count * lax.axis_size("seq")) ** (-0.5)
    taps_mr = mr_filter.astype(jnp.bfloat16)
    zero_taps = jnp.zeros_like(taps_mr)
    lower_band = toeplitz(jnp.concatenate([zero_taps, taps_mr], -1))
    upper_band = toeplitz(jnp.concatenate([taps_mr, zero_taps], -1))
    mixed_mr = (key_mr.astype(jnp.float32) * value_mr.astype(jnp.float32)).astype(jnp.bfloat16)
    rim_rows = from_behind(mixed_mr, "seq", 1)
    blocks = mixed_mr.reshape(block_count, tap_count, group_count, group_size)
    before = jnp.concatenate(
        [rim_rows.reshape(1, tap_count, group_count, group_size), blocks[:-1]], 0
    )
    conv_mr = jnp.einsum("gij,bjgc->bigc", lower_band, blocks, preferred_element_type=jnp.float32)
    conv_mr = conv_mr + jnp.einsum(
        "gij,bjgc->bigc", upper_band, before, preferred_element_type=jnp.float32
    )
    conv_mr = conv_mr.reshape(row_count, chan_count)
    out_mr = (query_mr.astype(jnp.float32) * conv_mr).astype(jnp.bfloat16)
    out_full = lax.optimization_barrier(out_mr).astype(jnp.float32)
    squares = lax.psum(jnp.sum(out_full * out_full, axis=1), "chan")
    inv_rms = lax.rsqrt(squares / D + 1e-06)[:, None]
    normed = out_full * inv_rms * norm_gain
    mixed_li = key_li.astype(jnp.float32) * normed
    cotan_full = cotangent.astype(jnp.float32)
    back_li = cotan_full * query_li.astype(jnp.float32)
    local_groups = group_count // lax.axis_size("seq")
    group_start = lax.axis_index("seq") * local_groups
    decays_here = lax.dynamic_slice_in_dim(li_decay, group_start, local_groups, 0)
    residues_here = lax.dynamic_slice_in_dim(li_residue, group_start, local_groups, 0)
    columns = lax.all_to_all(
        mixed_li.astype(jnp.bfloat16), "seq", split_axis=1, concat_axis=0, tiled=True
    ).astype(mixed_li.dtype)
    conv_li = lax.all_to_all(
        local_long(columns, decays_here, residues_here, False).astype(jnp.bfloat16),
        "seq",
        split_axis=0,
        concat_axis=1,
        tiled=True,
    ).astype(jnp.float32)
    grad_columns = lax.all_to_all(
        back_li.astype(jnp.bfloat16), "seq", split_axis=1, concat_axis=0, tiled=True
    ).astype(back_li.dtype)
    grad_mixed_li = lax.all_to_all(
        local_long(grad_columns, decays_here, residues_here, True),
        "seq",
        split_axis=0,
        concat_axis=1,
        tiled=True,
    )
    out_li = (query_li.astype(jnp.float32) * conv_li).astype(jnp.bfloat16)
    grad_query_li = (cotan_full * conv_li).astype(jnp.bfloat16)
    grad_key_li = (grad_mixed_li * normed).astype(jnp.bfloat16)
    grad_normed = grad_mixed_li * key_li.astype(jnp.float32)
    gain_part = jnp.sum(grad_normed * out_full * inv_rms, axis=0)
    weighted = grad_normed * norm_gain
    cross_dots = lax.psum(jnp.sum(weighted * out_full, axis=1), "chan")[:, None]
    grad_out_mr = inv_rms * weighted - out_full * inv_rms**3 * cross_dots / D
    grad_query_mr = (grad_out_mr * conv_mr).astype(jnp.bfloat16)
    back_mr = (grad_out_mr * query_mr.astype(jnp.float32)).astype(jnp.bfloat16)
    after_rim = from_behind(back_mr, "seq", -1)
    back_blocks = back_mr.reshape(block_count, tap_count, group_count, group_size)
    after_rows = jnp.concatenate(
        [back_blocks[1:], after_rim.reshape(1, tap_count, group_count, group_size)], 0
    )
    grad_mixed_mr = jnp.einsum(
        "gji,bjgc->bigc", lower_band, back_blocks, preferred_element_type=jnp.float32
    )
    grad_mixed_mr = grad_mixed_mr + jnp.einsum(
        "gji,bjgc->bigc", upper_band, after_rows, preferred_element_type=jnp.float32
    )
    grad_mixed_mr = grad_mixed_mr.reshape(row_count, chan_count)
    grad_key_mr = (grad_mixed_mr * value_mr.astype(jnp.float32)).astype(jnp.bfloat16)
    grad_value_mr = (grad_mixed_mr * key_mr.astype(jnp.float32)).astype(jnp.bfloat16)
    extended = jnp.concatenate([before, blocks], 1)
    gram_block = jnp.einsum(
        "bigc,bmgc->gim", back_blocks, extended, preferred_element_type=jnp.float32
    )
    flipped = jnp.flip(gram_block, -1)
    padded = jnp.pad(flipped, ((0, 0), (0, 0), (0, 1)))
    flattened = padded.reshape(group_count, -1)
    skewed = flattened[:, tap_count - 1 : tap_count - 1 + 2 * tap_count * tap_count]
    skewed = skewed.reshape(group_count, tap_count, 2 * tap_count)[:, :, :tap_count]
    filter_part = jnp.sum(skewed, axis=1)
    param_sums = (
        lax.psum(gain_part.astype(jnp.bfloat16), "seq").astype(jnp.float32),
        lax.psum(filter_part.astype(jnp.bfloat16), "seq").astype(jnp.float32),
    )
    grad_gain = param_sums[0] * grad_scale
    grad_filter = param_sums[1] * grad_scale
    return (
        out_li,
        grad_query_mr,
        grad_key_mr,
        grad_value_mr,
        grad_query_li,
        grad_key_li,
        grad_gain,
        grad_filter,
    )


def solution(mesh):
    in_specs = (
        P("seq", "chan"),
        P("seq", "chan"),
        P("seq", "chan"),
        P("seq", "chan"),
        P("seq", "chan"),
        P("seq", "chan"),
        P("chan", None),
        P("chan"),
        P("chan", None),
        P("chan", None),
    )
    out_specs = (
        P("seq", "chan"),
        P("seq", "chan"),
        P("seq", "chan"),
        P("seq", "chan"),
        P("seq", "chan"),
        P("seq", "chan"),
        P("chan"),
        P("chan", None),
    )
    return jax.shard_map(
        on_device, mesh=mesh, in_specs=in_specs, out_specs=out_specs, check_vma=False
    )
```

profile of v0, /device:TPU:32, one launch (start us, length us, event | category | flops | bytes accessed | tf_op | source)
XLA Modules:
  0.0 443.5 jit_solution(472008142492113452)
XLA Ops:
  3.7 11.5 %all-to-all-start.2 = ((bf16[128,32,32]{0,2,1:T(8,128)(2,1)}), bf16[128,32,32]{0,2,1:T(8,128)(2,1)S(1)}, u32[]{:S(2)}, u32[]{:S(2)}) async-start(bf16[128,32,32]{0,2,1:T(8,128)(2,1)} %bitcast.30), calls=%async_computation.2 | async-start | bytes 524288 | tf_op jit(solution)/shard_map/all_to_all | solution.py:132
  17.6 3.4 collective-permute-start
  34.2 2.6 copy.273
  39.0 15.9 %reshape.167 = bf16[64,128,255]{2,1,0:T(8,128)(2,1)} reshape(bf16[64,32640]{1,0:T(8,128)(2,1)} %slice.458) | data formatting | bytes 8355840 | tf_op jit(solution)/shard_map/reshape | solution.py:25
  55.2 2.6 copy.274
  60.0 15.9 %reshape.169 = bf16[64,128,255]{2,1,0:T(8,128)(2,1)} reshape(bf16[64,32640]{1,0:T(8,128)(2,1)} %slice.460) | data formatting | bytes 8355840 | tf_op jit(solution)/shard_map/reshape | solution.py:25
  77.0 3.6 fusion.6
  86.6 11.2 %pad.305 = f32[32,2,16,16]{2,3,0,1:T(8,128)S(1)} pad(f32[16,2,16,16]{2,3,0,1:T(8,128)} %add.314, f32[]{:T(128)} %constant.15.clone.1), padding=1_0_1x0_0_0x0_0_0x0_0_0 | pad | bytes 98308
  103.5 8.9 %all-to-all-start.3 = ((f32[32,128,32]{1,2,0:T(8,128)}), f32[32,128,32]{1,2,0:T(8,128)S(1)}, u32[]{:S(2)}, u32[]{:S(2)}) async-start(f32[32,128,32]{1,2,0:T(8,128)} %bitcast.140), calls=%async_computation.3 | async-start | bytes 1048576 | tf_op jit(solution)/shard_map/all_to_all | solution.py:135
  112.4 2.9 fusion.8
  115.6 13.8 %psum.28 = f32[128]{0:T(128)S(1)} all-reduce(f32[128]{0:T(128)S(1)} %fusion.26), channel_id=1, replica_groups=mesh['seq'=32,'chan'=8] {'chan'}, use_global_device_ids=true, to_apply=%region_1.2 | all-reduce | flops 128 | bytes 1024 | tf_op jit(solution)/shard_map/psum | solution.py:112
  129.8 12.4 %psum.29 = f32[128]{0:T(128)S(1)} all-reduce(f32[128]{0:T(128)S(1)} %get-tuple-element.49), channel_id=1, replica_groups=mesh['seq'=32,'chan'=8] {'chan'}, use_global_device_ids=true, to_apply=%region_3.4 | all-reduce | flops 128 | bytes 1024 | tf_op jit(solution)/shard_map/psum | solution.py:148
  145.2 9.5 %all-to-all-start = ((bf16[128,32,32]{0,2,1:T(8,128)(2,1)}), bf16[128,32,32]{0,2,1:T(8,128)(2,1)S(1)}, u32[]{:S(2)}, u32[]{:S(2)}) async-start(bf16[128,32,32]{0,2,1:T(8,128)(2,1)} %bitcast.141), calls=%async_computation | async-start | bytes 524288 | tf_op jit(solution)/shard_map/all_to_all | solution.py:122
  158.7 5.5 %fusion.36 = f32[64,128,256]{2,1,0:T(8,128)} fusion(bf16[128,64,16]{0,2,1:T(8,128)(2,1)S(1)} %bitcast.138, bf16[1,128,64,16]{1,3,2,0:T(8,128)(2,1)S(1)} %bitcast.137, bf16[1,128,64,16]{1,3,2,0:T(8,128)(2,1)} %bitcast.55), kind=kOutput, calls=%fused_computation.53 | convolution fusion | flops 68157440 | bytes 9175040 | tf_op jit(solution)/shard_map/bigc,bmgc->gim/dot_general | solution.py:167
  164.2 67.4 %rev.14 = f32[64,128,256]{2,1,0:T(8,128)} reverse(f32[64,128,256]{2,1,0:T(8,128)} %fusion.36), dimensions={2} | reverse | bytes 16777216 | tf_op jit(solution)/shard_map/jit(_flip)/rev | solution.py:170
  231.5 9.6 %pad.177 = f32[64,128,257]{2,1,0:T(8,128)} pad(f32[64,128,256]{2,1,0:T(8,128)} %rev.14, f32[]{:T(128)} %constant.15.clone.1), padding=0_0x0_0x0_1 | pad | bytes 16809988 | tf_op jit(solution)/shard_map/jit(_pad)/pad | solution.py:171
  241.1 12.2 %reshape.180 = f32[64,32896]{1,0:T(8,128)} reshape(f32[64,128,257]{2,1,0:T(8,128)} %pad.177) | data formatting | bytes 16842752 | tf_op jit(solution)/shard_map/reshape | solution.py:172
  253.3 5.6 %slice.516 = f32[64,32768]{1,0:T(8,128)S(1)} slice(f32[64,32896]{1,0:T(8,128)} %reshape.180), slice={[0:64], [127:32895]} | slice | bytes 16777216 | tf_op jit(solution)/shard_map/slice | solution.py:173
  258.9 2.5 copy.276
  262.0 139.5 %all-reduce.49 = (bf16[1024]{0:T(1024)(128)(2,1)S(1)}, bf16[64,128]{1,0:T(8,128)(2,1)S(1)}) all-reduce(bf16[1024]{0:T(1024)(128)(2,1)S(1)} %get-tuple-element.48, bf16[64,128]{1,0:T(8,128)(2,1)S(1)} %slice_reduce_fusion), channel_id=1, replica_groups=mesh['seq'=32,'chan'=8] {'seq'}, use_global_device_ids=true, to_apply=%region_5.6 | all-reduce | flops 9216 | bytes 36864 | tf_op jit(solution)/shard_map/psum | solution.py:177
  407.5 11.2 %pad.303 = f32[32,2,16,16]{2,3,0,1:T(8,128)S(1)} pad(f32[16,2,16,16]{2,3,0,1:T(8,128)} %add.291, f32[]{:T(128)} %constant.15.clone.1), padding=1_0_1x0_0_0x0_0_0x0_0_0 | pad | bytes 98308
  421.5 9.1 %all-to-all-start.1 = ((bf16[32,128,32]{1,2,0:T(8,128)(2,1)}), bf16[32,128,32]{1,2,0:T(8,128)(2,1)S(1)}, u32[]{:S(2)}, u32[]{:S(2)}) async-start(bf16[32,128,32]{1,2,0:T(8,128)(2,1)} %bitcast.27), calls=%async_computation.1 | async-start | bytes 524288 | tf_op jit(solution)/shard_map/all_to_all | solution.py:125
  430.6 2.3 fusion.11
  434.8 6.9 %all-to-all-done.1 = bf16[32,128,32]{1,2,0:T(8,128)(2,1)S(1)} async-done(((bf16[32,128,32]{1,2,0:T(8,128)(2,1)}), bf16[32,128,32]{1,2,0:T(8,128)(2,1)S(1)}, u32[]{:S(2)}, u32[]{:S(2)}) %all-to-all-start.1) | async-done | bytes 262176 | tf_op jit(solution)/shard_map/all_to_all | solution.py:125
  (234 shorter events, 55.9 us)
Async XLA Ops:
  0.6 20.3 %copy-start.10 = (f32[64,16]{0,1:T(8,128)S(1)}, f32[64,16]{0,1:T(8,128)}, u32[]{:S(2)}) copy-start(f32[64,16]{0,1:T(8,128)} %param.19) | copy-start | bytes 12292
  0.6 20.3 %copy-start.9 = (f32[64,16]{0,1:T(8,128)S(1)}, f32[64,16]{0,1:T(8,128)}, u32[]{:S(2)}) copy-start(f32[64,16]{0,1:T(8,128)} %param.18) | copy-start | bytes 12292
  0.7 29.6 %copy-start.3 = (f32[64,128]{1,0:T(8,128)S(1)}, f32[64,128]{1,0:T(8,128)}, u32[]{:S(2)}) copy-start(f32[64,128]{1,0:T(8,128)} %param.16) | copy-start | bytes 98308
  2.9 30.5 %copy-start.1 = (bf16[128,1024]{1,0:T(8,128)(2,1)S(1)}, bf16[128,1024]{1,0:T(8,128)(2,1)}, u32[]{:S(2)}) copy-start(bf16[128,1024]{1,0:T(8,128)(2,1)} %param.10) | copy-start | bytes 786436
  3.7 29.9 %copy-start.2 = (bf16[128,1024]{1,0:T(8,128)(2,1)S(1)}, bf16[128,1024]{1,0:T(8,128)(2,1)}, u32[]{:S(2)}) copy-start(bf16[128,1024]{1,0:T(8,128)(2,1)} %param.14) | copy-start | bytes 786436
  3.7 76.9 %all-to-all-start.2 = ((bf16[128,32,32]{0,2,1:T(8,128)(2,1)}), bf16[128,32,32]{0,2,1:T(8,128)(2,1)S(1)}, u32[]{:S(2)}, u32[]{:S(2)}) async-start(bf16[128,32,32]{0,2,1:T(8,128)(2,1)} %bitcast.30), calls=%async_computation.2 | async-start | bytes 524288 | tf_op jit(solution)/shard_map/all_to_all | solution.py:132
  17.6 94.9 %collective-permute-start = (bf16[128,1024]{0,1:T(8,128)(2,1)S(1)}, bf16[128,1024]{0,1:T(8,128)(2,1)}, u32[]{:S(2)}, u32[]{:S(2)}) collective-permute-start(bf16[128,1024]{0,1:T(8,128)(2,1)S(1)} %fusion.22), channel_id=1, source_target_pairs={{0,8},{8,16},{16,24},{24,32},{32,40},{40,48},{48,56},{56,64},{64,7... | collective-permute-start | bytes 786440 | tf_op jit(solution)/shard_map/ppermute | solution.py:17
  21.8 7.3 %copy-start.6 = (f32[2,16]{1,0:T(2,128)}, f32[2,16]{1,0:T(2,128)S(1)}, u32[]{:S(2)}) copy-start(f32[2,16]{1,0:T(2,128)S(1)} %get-tuple-element.92) | copy-start | bytes 388
  33.4 67.1 %copy-start = (f32[2,128,255]{2,1,0:T(8,128)}, f32[2,128,255]{2,1,0:T(8,128)S(1)}, u32[]{:S(2)}) copy-start(f32[2,128,255]{2,1,0:T(8,128)S(1)} %reshape.172) | copy-start | bytes 783364
  85.1 15.8 %copy-start.7 = (f32[2,16]{1,0:T(2,128)S(1)}, f32[2,16]{1,0:T(2,128)}, u32[]{:S(2)}) copy-start(f32[2,16]{1,0:T(2,128)} %copy-done.6) | copy-start | bytes 388
  85.1 15.8 %copy-start.12 = (f32[128]{0:T(128)S(1)}, f32[128]{0:T(128)}, u32[]{:S(2)}) copy-start(f32[128]{0:T(128)} %iota_subtract_fusion) | copy-start | bytes 1540
  100.9 28.4 %copy-start.4 = (f32[1024]{0:T(1024)S(1)}, f32[1024]{0:T(1024)}, u32[]{:S(2)}) copy-start(f32[1024]{0:T(1024)} %param.17) | copy-start | bytes 12292
  103.5 25.9 %all-to-all-start.3 = ((f32[32,128,32]{1,2,0:T(8,128)}), f32[32,128,32]{1,2,0:T(8,128)S(1)}, u32[]{:S(2)}, u32[]{:S(2)}) async-start(f32[32,128,32]{1,2,0:T(8,128)} %bitcast.140), calls=%async_computation.3 | async-start | bytes 1048576 | tf_op jit(solution)/shard_map/all_to_all | solution.py:135
  145.2 259.7 %all-to-all-start = ((bf16[128,32,32]{0,2,1:T(8,128)(2,1)}), bf16[128,32,32]{0,2,1:T(8,128)(2,1)S(1)}, u32[]{:S(2)}, u32[]{:S(2)}) async-start(bf16[128,32,32]{0,2,1:T(8,128)(2,1)} %bitcast.141), calls=%async_computation | async-start | bytes 524288 | tf_op jit(solution)/shard_map/all_to_all | solution.py:122
  156.5 274.1 %collective-permute-start.1 = (bf16[128,1024]{0,1:T(8,128)(2,1)S(1)}, bf16[128,1024]{0,1:T(8,128)(2,1)}, u32[]{:S(2)}, u32[]{:S(2)}) collective-permute-start(bf16[128,1024]{0,1:T(8,128)(2,1)S(1)} %get-tuple-element.52), channel_id=1, source_target_pairs={{8,0},{16,8},{24,16},{32,24},{40,32},{48,40},{56,48},{64,56},{72,6... | collective-permute-start | bytes 786440 | tf_op jit(solution)/shard_map/ppermute | solution.py:17
  261.4 143.5 %copy-start.13 = (f32[128]{0:T(128)S(1)}, f32[128]{0:T(128)}, u32[]{:S(2)}) copy-start(f32[128]{0:T(128)} %iota_subtract_fusion.1) | copy-start | bytes 1540
  261.5 144.1 %copy-start.5 = (f32[2,16]{1,0:T(2,128)S(1)}, f32[2,16]{1,0:T(2,128)}, u32[]{:S(2)}) copy-start(f32[2,16]{1,0:T(2,128)} %get-tuple-element.82) | copy-start | bytes 388
  261.5 144.1 %copy-start.11 = (f32[2,16]{1,0:T(2,128)S(1)}, f32[2,16]{1,0:T(2,128)}, u32[]{:S(2)}) copy-start(f32[2,16]{1,0:T(2,128)} %get-tuple-element.89) | copy-start | bytes 388
  405.9 14.3 %copy-start.8 = (f32[2,16]{1,0:T(2,128)S(1)}, f32[2,16]{1,0:T(2,128)}, u32[]{:S(2)}) copy-start(f32[2,16]{1,0:T(2,128)} %copy-done.6) | copy-start | bytes 388
  421.5 20.2 %all-to-all-start.1 = ((bf16[32,128,32]{1,2,0:T(8,128)(2,1)}), bf16[32,128,32]{1,2,0:T(8,128)(2,1)S(1)}, u32[]{:S(2)}, u32[]{:S(2)}) async-start(bf16[32,128,32]{1,2,0:T(8,128)(2,1)} %bitcast.27), calls=%async_computation.1 | async-start | bytes 524288 | tf_op jit(solution)/shard_map/all_to_all | solution.py:125
where the time goes:
time: 451 us; the launch traced here: 444 us
  local copies, waits for them, and re-layouts  188 us (42%)
  blocking collectives  166 us (37%)
  starting transfers between devices  44.5 us (10%)
  matrix products  21.6 us (5%)
  other arithmetic  15.6 us (3%)
  waiting for transfers between devices  6.91 us (2%)
    psum x1, blocking collectives, on_device(): lax.psum(gain_part.astype(jnp.bfloat16), 'seq').astype(jnp.float32)  139 us
    rev x1, local copies, waits for them, and re-layouts, on_device(): flipped = jnp.flip(gram_block, -1)  67.4 us
    unnamed x57, local copies, waits for them, and re-layouts  43.6 us
    reshape x3, local copies, waits for them, and re-layouts, toeplitz(): repeated[:, :block_len * (double_len - 1)]  32.2 us
    psum x1, blocking collectives, on_device(): squares = lax.psum(jnp.sum(out_full * out_full, axis=1), 'chan')  13.8 us
    psum x1, blocking collectives, on_device(): cross_dots = lax.psum(jnp.sum(weighted * out_full, axis=1), 'chan')[:, None]  12.4 us
    reshape x1, local copies, waits for them, and re-layouts, on_device(): flattened = padded.reshape(group_count, -1)  12.2 us
    all_to_all x1, starting transfers between devices, on_device(): lax.all_to_all(back_li.astype(jnp.bfloat16), 'seq', split_axis=1, concat_...  11.5 us
  transfers between devices with their start and end apart: 6, of which 1 were waited for; matrix products, arithmetic and copies ran while one was open for 49% of the time, Pallas kernels for 0%

commit v1 on v0

v1 whole, which is shorter than its diff:
```python
import functools

import jax
import jax.numpy as jnp
from jax import lax
from jax.experimental import pallas as pl
from jax.experimental.pallas import tpu as pltpu
from jax.sharding import PartitionSpec as P

MESH = pl.DeviceIdType.MESH
F32 = jnp.float32
BF16 = jnp.bfloat16
B = 128
GS = 16
GT = B // GS


def dot(a, b):
    return jnp.dot(a, b, preferred_element_type=F32)


def split(x):
    hi = x.astype(BF16)
    return hi, (x - hi.astype(F32)).astype(BF16)


def kernel(
    n_seq, n_chan, nt,
    q_mr, k_mr, v_mr, q_li, k_li, cot, filt, gain, decay, resid,
    out_li, g_qmr, g_kmr, g_vmr, g_qli, g_kli, g_gain, g_filt,
    ext, bext, tmf, tmb, tlf, tlb, conv, outm, gml, bli, xli, cli,
    winf, winb, woutf, woutb, taps, rtaps, avec,
    bs_src, bs_dst, be_src, be_dst, fs_src, fs_dst, fe_src, fe_dst,
    pbuf, r_src, r_dst, a_src, a_dst,
    hf_s, hf_r, hb_s, hb_r, bs_s, bs_r, be_s, be_r, fs_s, fs_r, fe_s, fe_r,
    p_s, p_r, r_s, r_r, a_s, a_r,
):
    seq = lax.axis_index("seq")
    chan = lax.axis_index("chan")
    units = 2 * nt
    total = float(n_chan * nt * B)
    scale = float(n_seq * B) ** -0.5
    base_b, base_f, base_r = 0, n_seq - units, 0

    lane = lax.broadcasted_iota(jnp.int32, (B, B), 1)
    row = lax.broadcasted_iota(jnp.int32, (B, B), 0)
    lane_group = lane >> 4
    diag_groups = (row >> 4) == lane_group
    eye = row == lane

    def cols(k):
        return pl.ds(pl.multiple_of(k * B, B), B)

    def tile(ref, k):
        return ref[:, cols(k)].astype(F32)

    def pick(stacked):
        out = stacked[0:B]
        for g in range(1, GT):
            out = jnp.where(lane_group == g, stacked[g * B:(g + 1) * B], out)
        return out

    def squeeze(full):
        return jnp.sum(jnp.where(diag_groups, full, 0.0).reshape(GT, GS, B), axis=0)

    def remote(src, dst, ss, rs, axis, target):
        return pltpu.make_async_remote_copy(
            src_ref=src, dst_ref=dst, send_sem=ss, recv_sem=rs,
            device_id={axis: target}, device_id_type=MESH,
        )

    barrier = pltpu.get_barrier_semaphore()

    @pl.loop(1, n_seq)
    def _(d):
        pl.semaphore_signal(barrier, inc=1, device_id={"seq": lax.rem(seq + d, n_seq)}, device_id_type=MESH)

    @pl.loop(1, n_chan)
    def _(d):
        pl.semaphore_signal(barrier, inc=1, device_id={"chan": lax.rem(chan + d, n_chan)}, device_id_type=MESH)

    @pl.loop(0, nt)
    def _(k):
        ext[k, 0:B, :] = (tile(k_mr, k) * tile(v_mr, k)).astype(BF16)

    pl.semaphore_wait(barrier, n_seq - 1 + n_chan - 1)

    def halo_f(k):
        return remote(ext.at[k, pl.ds(0, B)], ext.at[k, pl.ds(B, B)], hf_s.at[k], hf_r.at[k], "seq", lax.rem(seq + 1, n_seq))

    def halo_b(k):
        return remote(bext.at[k, pl.ds(0, B)], bext.at[k, pl.ds(B, B)], hb_s.at[k], hb_r.at[k], "seq",
                      lax.rem(seq + n_seq - 1, n_seq))

    @pl.when(seq < n_seq - 1)
    def _():
        @pl.loop(0, nt)
        def _(k):
            halo_f(k).start()

    @pl.when(seq == 0)
    def _():
        @pl.loop(0, nt)
        def _(k):
            ext[k, B:2 * B, :] = jnp.zeros((B, B), BF16)

    @pl.when(seq == n_seq - 1)
    def _():
        @pl.loop(0, nt)
        def _(k):
            bext[k, B:2 * B, :] = jnp.zeros((B, B), BF16)

    def scatter_copy(src, dst, ss, rs, base, u):
        return remote(src.at[u], dst.at[seq], ss.at[u], rs.at[seq], "seq", base + u)

    def scatter(src, dst, ss, rs, base, count):
        for u in range(count):
            @pl.when(seq != base + u)
            def _():
                scatter_copy(src, dst, ss, rs, base, u).start()

            @pl.when(seq == base + u)
            def _():
                dst[seq] = src[u]

    def scatter_wait(src, dst, ss, rs, base, count):
        for u in range(count):
            @pl.when(seq != base + u)
            def _():
                scatter_copy(src, dst, ss, rs, base, u).wait_send()

    def owner_wait(src, dst, ss, rs):
        @pl.loop(1, n_seq)
        def _(d):
            other = lax.rem(seq + d, n_seq)
            remote(src.at[0], dst.at[other], ss.at[0], rs.at[other], "seq", other).wait_recv()

    def answer_wait(src, dst, ss, rs, base, count):
        for u in range(count):
            @pl.when(seq != base + u)
            def _():
                remote(src.at[0], dst.at[u], ss.at[0], rs.at[u], "seq", base + u).wait_recv()

    def owns(base, count):
        return jnp.logical_and(seq >= base, seq < base + count)

    def owner_scan(src, dst, ss, rs, e_src, e_dst, es, er, base, backward):
        @pl.when(owns(base, units))
        def _():
            owner_wait(src, dst, ss, rs)
            u = seq - base
            fade = avec[u]

            def step(i, state):
                q = n_seq - 1 - i if backward else i
                e_src[q] = state
                return fade * state + dst[q]

            lax.fori_loop(0, n_seq, step, jnp.zeros((8, B), F32))
            e_dst[u] = e_src[seq]

            @pl.loop(1, n_seq)
            def _(d):
                other = lax.rem(seq + d, n_seq)
                remote(e_src.at[other], e_dst.at[u], es.at[other], er.at[u], "seq", other).start()

    def owner_sends_wait(e_src, e_dst, es, er, base, count, one):
        @pl.when(owns(base, count))
        def _():
            u = seq - base

            @pl.loop(1, n_seq)
            def _(d):
                other = lax.rem(seq + d, n_seq)
                src = e_src.at[0] if one else e_src.at[other]
                remote(src, e_dst.at[u], es.at[other], er.at[u], "seq", other).wait_send()

    eye_modes = lax.broadcasted_iota(jnp.int32, (GS, GS), 0) == lax.broadcasted_iota(jnp.int32, (GS, GS), 1)
    time = lane.astype(F32)

    @pl.loop(0, nt)
    def _(k):
        def column(ref):
            parts = []
            for g in range(GT):
                values = ref[pl.ds(k * GT + g, 1), :]
                parts.append(jnp.sum(jnp.where(eye_modes, values, 0.0), axis=1, keepdims=True))
            return jnp.concatenate(parts, axis=0)

        rate = column(decay)
        weight = column(resid) * jnp.sqrt(2.0 * rate)
        fading = jnp.exp(-rate * time)
        hi, lo = split(fading)
        winb[k, 0:B, :] = hi
        winb[k, B:2 * B, :] = lo
        back = (tile(cot, k) * tile(q_li, k)).astype(BF16)
        bli[k] = back
        states = squeeze(dot(hi, back) + dot(lo, back))
        bs_src[2 * k] = states[0:8]
        bs_src[2 * k + 1] = states[8:16]
        powers = squeeze(jnp.broadcast_to(jnp.exp(-rate * float(B)), (B, B)))
        avec[2 * k] = powers[0:8]
        avec[2 * k + 1] = powers[8:16]
        taps[1, pl.ds(pl.multiple_of(k * GT, GT), GT), :] = jnp.sum((weight * fading).reshape(GT, GS, B), axis=1)
        hi, lo = split(jnp.exp(-rate * (B - 1.0 - time)))
        winf[k, 0:B, :] = hi
        winf[k, B:2 * B, :] = lo
        hi, lo = split((weight * jnp.exp(-rate * (B - time))).T)
        woutb[k, :, 0:B] = hi
        woutb[k, :, B:2 * B] = lo
        hi, lo = split((weight * jnp.exp(-rate * (time + 1.0))).T)
        woutf[k, :, 0:B] = hi
        woutf[k, :, B:2 * B] = lo

    scatter(bs_src, bs_dst, bs_s, bs_r, base_b, units)

    reflect = jnp.where(row == ((B - lane) & (B - 1)), 1.0, 0.0)
    taps[0] = filt[...].astype(BF16).astype(F32)
    for which in range(2):
        rtaps[which] = dot(taps[which].astype(BF16), reflect.astype(BF16))

    def rolled(ref, which, group):
        line = jnp.broadcast_to(ref[which, pl.ds(group, 1), :], (B, B))
        return pltpu.roll(line, 0, axis=1, stride=1, stride_axis=0)

    def build(ref, which, mask, out):
        @pl.loop(0, nt)
        def _(k):
            for g in range(GT):
                matrix = rolled(ref, which, k * GT + g)
                out[k, g * B:(g + 1) * B, 0:B] = jnp.where(mask, matrix, 0.0).astype(BF16)
                if which == 0:
                    out[k, g * B:(g + 1) * B, B:2 * B] = jnp.where(mask, 0.0, matrix).astype(BF16)

    build(rtaps, 0, lane <= row, tmf)
    build(taps, 1, lane >= row, tlb)

    owner_scan(bs_src, bs_dst, bs_s, bs_r, be_src, be_dst, be_s, be_r, base_b, True)

    def carried(wout, e_dst, k):
        state = jnp.concatenate([e_dst[2 * k], e_dst[2 * k + 1]], axis=0)
        hi, lo = split(jnp.where(diag_groups, jnp.concatenate([state] * GT, axis=0), 0.0))
        return dot(wout[k], jnp.concatenate([hi, hi], axis=0)) + dot(wout[k, :, 0:B], lo)

    @pl.loop(0, nt)
    def _(k):
        gml[k] = pick(dot(tlb[k], bli[k]))

    squares = jnp.zeros((B, B), F32)

    def mr_step(k, squares):
        @pl.when(seq > 0)
        def _():
            halo_f(k).wait_recv()

        value = pick(dot(tmf[k], ext[k]))
        conv[k] = value
        gated = (tile(q_mr, k) * value).astype(BF16).astype(F32)
        outm[k] = gated
        return squares + gated * gated

    squares = lax.fori_loop(0, nt, mr_step, squares)

    answer_wait(be_src, be_dst, be_s, be_r, base_b, units)

    def li_step(k, cross):
        grad = gml[k] + carried(woutb, be_dst, k)
        gml[k] = grad
        return cross + grad * tile(k_li, k) * outm[k] * gain[pl.ds(k, 1), :]

    cross = lax.fori_loop(0, nt, li_step, jnp.zeros((B, B), F32))

    def as_row(partial):
        column = jnp.sum(partial, axis=1, keepdims=True)
        return jnp.sum(jnp.where(eye, column, 0.0), axis=0, keepdims=True)

    def as_column(line):
        return jnp.sum(jnp.where(eye, line, 0.0), axis=1, keepdims=True)

    row8 = lax.broadcasted_iota(jnp.int32, (8, B), 0)
    pbuf[chan] = jnp.where(row8 == 0, as_row(squares), as_row(cross))

    def psum_copy(d):
        other = lax.rem(chan + d, n_chan)
        return remote(pbuf.at[chan], pbuf.at[chan], p_s.at[other], p_r.at[chan], "chan", other)

    @pl.loop(1, n_chan)
    def _(d):
        psum_copy(d).start()

    build(taps, 0, lane >= row, tmb)
    build(rtaps, 1, lane <= row, tlf)

    @pl.loop(1, n_chan)
    def _(d):
        other = lax.rem(chan + d, n_chan)
        remote(pbuf.at[other], pbuf.at[other], p_s.at[other], p_r.at[other], "chan", other).wait_recv()

    sums = pbuf[0]
    for c in range(1, n_chan):
        sums = sums + pbuf[c]
    inv_row = lax.rsqrt(sums[0:1] / total + 1e-06)
    inv = as_column(inv_row)
    pull = as_column(inv_row * inv_row * inv_row * sums[1:2] / total)

    @pl.loop(0, nt)
    def _(k):
        gated, grad, key = outm[k], gml[k], tile(k_li, k)
        gains = gain[pl.ds(k, 1), :]
        scaled = gated * inv
        normed = scaled * gains
        grad_normed = grad * key
        g_kli[:, cols(k)] = (grad * normed).astype(BF16)
        grad_out = inv * (grad_normed * gains) - gated * pull
        bext[k, 0:B, :] = (grad_out * tile(q_mr, k)).astype(BF16)

        @pl.when(seq > 0)
        def _():
            halo_b(k).start()

        g_qmr[:, cols(k)] = (grad_out * conv[k]).astype(BF16)
        r_src[nt, pl.ds(k, 1), :] = jnp.sum(grad_normed * scaled, axis=0, keepdims=True)
        mixed = (key * normed).astype(BF16)
        xli[k] = mixed
        both = dot(winf[k], mixed)
        states = squeeze(both[0:B] + both[B:2 * B])
        fs_src[2 * k] = states[0:8]
        fs_src[2 * k + 1] = states[8:16]

    if nt < 8:
        r_src[nt, nt:8, :] = jnp.zeros((8 - nt, B), F32)
    scatter(fs_src, fs_dst, fs_s, fs_r, base_f, units)

    row64 = lax.broadcasted_iota(jnp.int32, (8 * GT, B), 0)

    @pl.loop(0, nt)
    def _(k):
        back = bext[k, 0:B, :]
        masked = jnp.concatenate([jnp.where(lane_group == g, back, jnp.zeros_like(back)) for g in range(GT)], axis=0)
        gram = lax.dot_general(masked, ext[k], (((1,), (1,)), ((), ())), preferred_element_type=F32)
        sums = []
        for g in range(GT):
            rows = gram[g * B:(g + 1) * B]
            cyclic = jnp.where(lane <= row, rows[:, 0:B], rows[:, B:2 * B])
            acc = cyclic[B - 8:B]
            for b in range(B // 8 - 2, -1, -1):
                acc = pltpu.roll(acc, B - 8, axis=1) + cyclic[8 * b:8 * b + 8]
            sums.append(acc)
        acc = jnp.concatenate(sums, axis=0)
        for bit in range(3):
            acc = jnp.where(((row64 >> bit) & 1) == 1, pltpu.roll(acc, B - (1 << bit), axis=1), acc)
        diagonals = jnp.sum(acc.reshape(GT, 8, B), axis=1)
        hi = diagonals.astype(BF16)
        rest = diagonals - hi.astype(F32)
        mid, lo = split(rest)
        parts = dot(jnp.concatenate([hi.astype(F32), mid.astype(F32), lo.astype(F32)], axis=0).astype(BF16),
                    reflect.astype(BF16))
        r_src[k] = parts[0:8] + parts[8:16] + parts[16:24]

    scatter(r_src, r_dst, r_s, r_r, base_r, nt + 1)

    owner_scan(fs_src, fs_dst, fs_s, fs_r, fe_src, fe_dst, fe_s, fe_r, base_f, False)

    @pl.loop(0, nt)
    def _(k):
        cli[k] = pick(dot(tlf[k], xli[k]))

    @pl.when(owns(base_r, nt + 1))
    def _():
        owner_wait(r_src, r_dst, r_s, r_r)
        u = seq - base_r
        result = lax.fori_loop(1, n_seq, lambda q, acc: acc + r_dst[q], r_dst[0]) * scale
        a_src[0] = result
        a_dst[u] = result

        @pl.loop(1, n_seq)
        def _(d):
            other = lax.rem(seq + d, n_seq)
            remote(a_src.at[0], a_dst.at[u], a_s.at[other], a_r.at[u], "seq", other).start()

    answer_wait(fe_src, fe_dst, fe_s, fe_r, base_f, units)

    @pl.loop(0, nt)
    def _(k):
        value = cli[k] + carried(woutf, fe_dst, k)
        out_li[:, cols(k)] = (tile(q_li, k) * value).astype(BF16)
        g_qli[:, cols(k)] = (tile(cot, k) * value).astype(BF16)

    @pl.loop(0, nt)
    def _(k):
        @pl.when(seq < n_seq - 1)
        def _():
            halo_b(k).wait_recv()

        grad = pick(dot(tmb[k], bext[k]))
        g_kmr[:, cols(k)] = (grad * tile(v_mr, k)).astype(BF16)
        g_vmr[:, cols(k)] = (grad * tile(k_mr, k)).astype(BF16)

    answer_wait(a_src, a_dst, a_s, a_r, base_r, nt + 1)
    for k in range(nt):
        g_filt[k * 8:(k + 1) * 8, :] = a_dst[k]
    g_gain[...] = a_dst[nt, 0:nt, :]

    @pl.when(seq < n_seq - 1)
    def _():
        @pl.loop(0, nt)
        def _(k):
            halo_f(k).wait_send()

    @pl.when(seq > 0)
    def _():
        @pl.loop(0, nt)
        def _(k):
            halo_b(k).wait_send()

    scatter_wait(bs_src, bs_dst, bs_s, bs_r, base_b, units)
    scatter_wait(fs_src, fs_dst, fs_s, fs_r, base_f, units)
    scatter_wait(r_src, r_dst, r_s, r_r, base_r, nt + 1)
    owner_sends_wait(be_src, be_dst, be_s, be_r, base_b, units, False)
    owner_sends_wait(fe_src, fe_dst, fe_s, fe_r, base_f, units, False)
    owner_sends_wait(a_src, a_dst, a_s, a_r, base_r, nt + 1, True)

    @pl.loop(1, n_chan)
    def _(d):
        psum_copy(d).wait_send()


def solution(mesh):
    n_seq, n_chan = mesh.shape["seq"], mesh.shape["chan"]

    def on_device(q_mr, k_mr, v_mr, q_li, k_li, cot, filt, gain, decay, resid):
        rows, width = q_mr.shape
        nt = width // B
        units = 2 * nt
        wide = jax.ShapeDtypeStruct((rows, width), BF16)
        vmem = pl.BlockSpec(memory_space=pltpu.VMEM)
        dma = pltpu.SemaphoreType.DMA
        state = lambda count: pltpu.VMEM((count, 8, B), F32)
        plane = lambda kind: pltpu.VMEM((nt, B, B), kind)
        outs = pl.pallas_call(
            functools.partial(kernel, n_seq, n_chan, nt),
            out_shape=[wide] * 6 + [jax.ShapeDtypeStruct((nt, B), F32), jax.ShapeDtypeStruct(filt.shape, F32)],
            in_specs=[vmem] * 10,
            out_specs=[vmem] * 8,
            scratch_shapes=[
                pltpu.VMEM((nt, 2 * B, B), BF16), pltpu.VMEM((nt, 2 * B, B), BF16),
                pltpu.VMEM((nt, GT * B, 2 * B), BF16), pltpu.VMEM((nt, GT * B, 2 * B), BF16),
                pltpu.VMEM((nt, GT * B, B), BF16), pltpu.VMEM((nt, GT * B, B), BF16),
                plane(F32), plane(F32), plane(F32), plane(BF16), plane(BF16), plane(F32),
                pltpu.VMEM((nt, 2 * B, B), BF16), pltpu.VMEM((nt, 2 * B, B), BF16),
                pltpu.VMEM((nt, B, 2 * B), BF16), pltpu.VMEM((nt, B, 2 * B), BF16),
                pltpu.VMEM((2, nt * GT, B), F32), pltpu.VMEM((2, nt * GT, B), F32), state(units),
                state(units), state(n_seq), state(n_seq), state(units),
                state(units), state(n_seq), state(n_seq), state(units),
                state(n_chan), state(nt + 1), state(n_seq), state(1), state(nt + 1),
                dma((nt,)), dma((nt,)), dma((nt,)), dma((nt,)),
                dma((units,)), dma((n_seq,)), dma((n_seq,)), dma((units,)),
                dma((units,)), dma((n_seq,)), dma((n_seq,)), dma((units,)),
                dma((n_chan,)), dma((n_chan,)),
                dma((nt + 1,)), dma((n_seq,)), dma((n_seq,)), dma((nt + 1,)),
            ],
            compiler_params=pltpu.CompilerParams(
                collective_id=0, has_side_effects=True, vmem_limit_bytes=48 * 1024 * 1024
            ),
        )(q_mr, k_mr, v_mr, q_li, k_li, cot, filt, gain.reshape(nt, B), decay, resid)
        return (*outs[:6], outs[6].reshape(width), outs[7])

    wide, by_group, by_chan = P("seq", "chan"), P("chan", None), P("chan")
    return jax.shard_map(
        on_device, mesh=mesh,
        in_specs=(wide,) * 6 + (by_group, by_chan, by_group, by_group),
        out_specs=(wide,) * 6 + (by_chan, by_group),
        check_vma=False,
    )
```

time: 451 us -> 77.9 us (0.17); the launches traced: 444 us -> 77.2 us
  local copies, waits for them, and re-layouts: 188 us -> 12.6 us
  blocking collectives: 166 us -> 0 us
  Pallas kernels: 0 us -> 63.9 us
  starting transfers between devices: 44.5 us -> 0 us
  matrix products: 21.6 us -> 0 us
  other arithmetic: 15.6 us -> 0 us
  waiting for transfers between devices: 6.91 us -> 0 us
    psum x3 -> x0, blocking collectives: 166 us -> none  [the longest x1 139 us: on_device(): lax.psum(gain_part.astype(jnp.bfloat16), 'seq').astype(jnp.float32)]
    rev x1 -> x0, local copies, waits for them, and re-layouts: 67.4 us -> none  [on_device(): flipped = jnp.flip(gram_block, -1)]
    pallas_call x0 -> x1, Pallas kernels: none -> 63.9 us  [on_device(): pl.pallas_call(functools.partial(kernel, n_seq, n_chan, nt), out_shape=[w...]
    reshape x4 -> x0, local copies, waits for them, and re-layouts: 44.4 us -> none  [the longest x3 32.2 us: toeplitz(): repeated[:, :block_len * (double_len - 1)]]
    all_to_all x4 -> x0, starting transfers between devices: 39 us -> none  [the longest x1 11.5 us: on_device(): lax.all_to_all(back_li.astype(jnp.bfloat16), 'seq', split_axis=1, concat_...]
    unnamed x57 -> x28, local copies, waits for them, and re-layouts: 43.6 us -> 12.6 us
    dot_general x12 -> x0, matrix products: 21.6 us -> none  [the longest x1 5.47 us: on_device(): jnp.einsum('bigc,bmgc->gim', back_blocks, extended, preferred_element_typ...]
    slice x48 -> x0, local copies, waits for them, and re-layouts: 17.2 us -> none  [the longest x1 5.61 us: on_device(): flattened[:, tap_count - 1:tap_count - 1 + 2 * tap_count * tap_count]]
  transfers between devices with their start and end apart: 6 -> 0, of which waited for: 1 -> 0; matrix products, arithmetic and copies ran while one was open for 49% -> 0% of each run, Pallas kernels for 0% -> 0%
where the time goes in v1:
time: 77.9 us; the launch traced here: 77.2 us
  Pallas kernels  63.9 us (82%)
  local copies, waits for them, and re-layouts  12.6 us (16%)
    pallas_call x1, Pallas kernels, on_device(): pl.pallas_call(functools.partial(kernel, n_seq, n_chan, nt), out_shape=[w...  63.9 us
    unnamed x28, local copies, waits for them, and re-layouts  12.6 us

profile of v1, /device:TPU:32, one launch (start us, length us, event | category | flops | bytes accessed | tf_op | source)
XLA Modules:
  0.0 77.2 jit_solution(4647137462537036821)
XLA Ops:
  0.6 0.0 copy-start.8
  0.6 0.0 copy-start.6
  0.7 0.8 %copy.18.decay = f32[64,16]{1,0:T(8,128)S(1)} copy(f32[64,16]{0,1:T(8,128)} %param.18) | data formatting | bytes 8192 | tf_op args[8]
  1.4 0.0 copy-done.8
  1.4 0.0 copy-start.7
  1.5 0.1 copy.19.resid
  1.5 0.0 copy-done.6
  1.5 0.6 copy-done.7
  2.1 0.0 copy-start
  2.1 0.9 %copy-done = bf16[128,1024]{1,0:T(8,128)(2,1)S(1)} copy-done((bf16[128,1024]{1,0:T(8,128)(2,1)S(1)}, bf16[128,1024]{1,0:T(8,128)(2,1)}, u32[]{:S(2)}) %copy-start) | copy-done | bytes 262168
  3.1 0.9 %copy-done.1 = bf16[128,1024]{1,0:T(8,128)(2,1)S(1)} copy-done((bf16[128,1024]{1,0:T(8,128)(2,1)S(1)}, bf16[128,1024]{1,0:T(8,128)(2,1)}, u32[]{:S(2)}) %copy-start.1) | copy-done | bytes 262168
  4.0 0.9 %copy-done.2 = bf16[128,1024]{1,0:T(8,128)(2,1)S(1)} copy-done((bf16[128,1024]{1,0:T(8,128)(2,1)S(1)}, bf16[128,1024]{1,0:T(8,128)(2,1)}, u32[]{:S(2)}) %copy-start.2) | copy-done | bytes 262168
  5.0 0.9 %copy-done.3 = bf16[128,1024]{1,0:T(8,128)(2,1)S(1)} copy-done((bf16[128,1024]{1,0:T(8,128)(2,1)S(1)}, bf16[128,1024]{1,0:T(8,128)(2,1)}, u32[]{:S(2)}) %copy-start.3) | copy-done | bytes 262168
  5.9 0.9 %copy-done.4 = bf16[128,1024]{1,0:T(8,128)(2,1)S(1)} copy-done((bf16[128,1024]{1,0:T(8,128)(2,1)S(1)}, bf16[128,1024]{1,0:T(8,128)(2,1)}, u32[]{:S(2)}) %copy-start.4) | copy-done | bytes 262168
  6.9 0.9 %copy-done.5 = bf16[128,1024]{1,0:T(8,128)(2,1)S(1)} copy-done((bf16[128,1024]{1,0:T(8,128)(2,1)S(1)}, bf16[128,1024]{1,0:T(8,128)(2,1)}, u32[]{:S(2)}) %copy-start.5) | copy-done | bytes 262168
  7.8 63.9 %shard_map.161 = (bf16[128,1024]{1,0:T(8,128)(2,1)S(1)}, bf16[128,1024]{1,0:T(8,128)(2,1)S(1)}, bf16[128,1024]{1,0:T(8,128)(2,1)S(1)}, bf16[128,1024]{1,0:T(8,12...) custom-call(bf16[128,1024]{1,0:T(8,128)(2,1)S(1)} %copy-done, ...), custom_call_target="tpu_custom_call" | custom-call | tf_op jit(solution)/shard_map/pallas_call | solution.py:440
  71.8 0.7 copy.28
  72.5 0.7 copy.29
  73.2 0.7 copy.30
  73.9 0.7 copy.31
  74.6 0.7 copy.32
  75.3 0.7 copy.33
  76.0 0.6 copy.34
  76.6 0.6 copy.35
  (5 shorter events, 0.0 us)
Async XLA Ops:
  0.6 0.8 %copy-start.8 = (f32[64,16]{0,1:T(8,128)S(1)}, f32[64,16]{0,1:T(8,128)}, u32[]{:S(2)}) copy-start(f32[64,16]{0,1:T(8,128)} %param.19) | copy-start | bytes 12292
  0.6 0.9 %copy-start.6 = (f32[64,128]{1,0:T(8,128)S(1)}, f32[64,128]{1,0:T(8,128)}, u32[]{:S(2)}) copy-start(f32[64,128]{1,0:T(8,128)} %filt.1) | copy-start | bytes 98308
  1.4 0.7 copy-start.7
  2.1 0.9 %copy-start = (bf16[128,1024]{1,0:T(8,128)(2,1)S(1)}, bf16[128,1024]{1,0:T(8,128)(2,1)}, u32[]{:S(2)}) copy-start(bf16[128,1024]{1,0:T(8,128)(2,1)} %q_mr.1) | copy-start | bytes 786436
  3.1 0.9 %copy-start.1 = (bf16[128,1024]{1,0:T(8,128)(2,1)S(1)}, bf16[128,1024]{1,0:T(8,128)(2,1)}, u32[]{:S(2)}) copy-start(bf16[128,1024]{1,0:T(8,128)(2,1)} %k_mr.1) | copy-start | bytes 786436
  4.0 0.9 %copy-start.2 = (bf16[128,1024]{1,0:T(8,128)(2,1)S(1)}, bf16[128,1024]{1,0:T(8,128)(2,1)}, u32[]{:S(2)}) copy-start(bf16[128,1024]{1,0:T(8,128)(2,1)} %v_mr.1) | copy-start | bytes 786436
  5.0 0.9 %copy-start.3 = (bf16[128,1024]{1,0:T(8,128)(2,1)S(1)}, bf16[128,1024]{1,0:T(8,128)(2,1)}, u32[]{:S(2)}) copy-start(bf16[128,1024]{1,0:T(8,128)(2,1)} %q_li.1) | copy-start | bytes 786436
  5.9 0.9 %copy-start.4 = (bf16[128,1024]{1,0:T(8,128)(2,1)S(1)}, bf16[128,1024]{1,0:T(8,128)(2,1)}, u32[]{:S(2)}) copy-start(bf16[128,1024]{1,0:T(8,128)(2,1)} %k_li.1) | copy-start | bytes 786436
  6.9 0.9 %copy-start.5 = (bf16[128,1024]{1,0:T(8,128)(2,1)S(1)}, bf16[128,1024]{1,0:T(8,128)(2,1)}, u32[]{:S(2)}) copy-start(bf16[128,1024]{1,0:T(8,128)(2,1)} %cot.1) | copy-start | bytes 786436

commit v2 on v1

--- a/solution.py
+++ b/solution.py
@@ -26,13 +26,14 @@
 
 def kernel(
     n_seq, n_chan, nt,
+    q_mr_in, k_mr_in, v_mr_in, q_li_in, k_li_in, cot_in, filt_in, gain_in, decay_in, resid_in,
+    out_li, g_qmr, g_kmr, g_vmr, g_qli, g_kli, g_gain, g_filt,
     q_mr, k_mr, v_mr, q_li, k_li, cot, filt, gain, decay, resid,
-    out_li, g_qmr, g_kmr, g_vmr, g_qli, g_kli, g_gain, g_filt,
     ext, bext, tmf, tmb, tlf, tlb, conv, outm, gml, bli, xli, cli,
     winf, winb, woutf, woutb, taps, rtaps, avec,
     bs_src, bs_dst, be_src, be_dst, fs_src, fs_dst, fe_src, fe_dst,
     pbuf, r_src, r_dst, a_src, a_dst,
-    hf_s, hf_r, hb_s, hb_r, bs_s, bs_r, be_s, be_r, fs_s, fs_r, fe_s, fe_r,
+    in_sem, hf_s, hf_r, hb_s, hb_r, bs_s, bs_r, be_s, be_r, fs_s, fs_r, fe_s, fe_r,
     p_s, p_r, r_s, r_r, a_s, a_r,
 ):
     seq = lax.axis_index("seq")
@@ -69,6 +70,14 @@
             device_id={axis: target}, device_id_type=MESH,
         )
 
+    fetched = (k_mr, v_mr, decay, resid, cot, q_li, filt, gain, q_mr, k_li)
+    fetches = [
+        pltpu.make_async_copy(src, dst, in_sem.at[i])
+        for i, (src, dst) in enumerate(zip(
+            (k_mr_in, v_mr_in, decay_in, resid_in, cot_in, q_li_in, filt_in, gain_in, q_mr_in, k_li_in), fetched))
+    ]
+    for fetch in fetches:
+        fetch.start()
     barrier = pltpu.get_barrier_semaphore()
 
     @pl.loop(1, n_seq)
@@ -79,6 +88,9 @@
     def _(d):
         pl.semaphore_signal(barrier, inc=1, device_id={"chan": lax.rem(chan + d, n_chan)}, device_id_type=MESH)
 
+    fetches[0].wait()
+    fetches[1].wait()
+
     @pl.loop(0, nt)
     def _(k):
         ext[k, 0:B, :] = (tile(k_mr, k) * tile(v_mr, k)).astype(BF16)
@@ -86,10 +98,10 @@
     pl.semaphore_wait(barrier, n_seq - 1 + n_chan - 1)
 
     def halo_f(k):
-        return remote(ext.at[k, pl.ds(0, B)], ext.at[k, pl.ds(B, B)], hf_s.at[k], hf_r.at[k], "seq", lax.rem(seq + 1, n_seq))
+        return remote(ext.at[k, pl.ds(0, B)], ext.at[k, pl.ds(B, B)], hf_s, hf_r.at[k], "seq", lax.rem(seq + 1, n_seq))
 
     def halo_b(k):
-        return remote(bext.at[k, pl.ds(0, B)], bext.at[k, pl.ds(B, B)], hb_s.at[k], hb_r.at[k], "seq",
+        return remote(bext.at[k, pl.ds(0, B)], bext.at[k, pl.ds(B, B)], hb_s, hb_r.at[k], "seq",
                       lax.rem(seq + n_seq - 1, n_seq))
 
     @pl.when(seq < n_seq - 1)
@@ -110,44 +122,50 @@
         def _(k):
             bext[k, B:2 * B, :] = jnp.zeros((B, B), BF16)
 
-    def scatter_copy(src, dst, ss, rs, base, u):
-        return remote(src.at[u], dst.at[seq], ss.at[u], rs.at[seq], "seq", base + u)
+    def owns(base, count):
+        return jnp.logical_and(seq >= base, seq < base + count)
 
     def scatter(src, dst, ss, rs, base, count):
         for u in range(count):
             @pl.when(seq != base + u)
             def _():
-                scatter_copy(src, dst, ss, rs, base, u).start()
+                remote(src.at[u], dst.at[seq], ss, rs, "seq", base + u).start()
 
             @pl.when(seq == base + u)
             def _():
                 dst[seq] = src[u]
 
-    def scatter_wait(src, dst, ss, rs, base, count):
-        for u in range(count):
-            @pl.when(seq != base + u)
-            def _():
-                scatter_copy(src, dst, ss, rs, base, u).wait_send()
-
-    def owner_wait(src, dst, ss, rs):
+    def answer(e_src, e_dst, es, er, u, one):
         @pl.loop(1, n_seq)
         def _(d):
             other = lax.rem(seq + d, n_seq)
-            remote(src.at[0], dst.at[other], ss.at[0], rs.at[other], "seq", other).wait_recv()
-
-    def answer_wait(src, dst, ss, rs, base, count):
-        for u in range(count):
-            @pl.when(seq != base + u)
-            def _():
-                remote(src.at[0], dst.at[u], ss.at[0], rs.at[u], "seq", base + u).wait_recv()
-
-    def owns(base, count):
-        return jnp.logical_and(seq >= base, seq < base + count)
-
-    def owner_scan(src, dst, ss, rs, e_src, e_dst, es, er, base, backward):
+            remote(e_src.at[0] if one else e_src.at[other], e_dst.at[u], es, er, "seq", other).start()
+
+    def several(ref, ss, rs, count):
+        return remote(ref.at[pl.ds(0, count)], ref.at[pl.ds(0, count)], ss, rs, "seq", lax.rem(seq + 1, n_seq))
+
+    def but_own(base, count, wait):
+        @pl.when(owns(base, count))
+        def _():
+            wait(count - 1)
+
+        @pl.when(jnp.logical_not(owns(base, count)))
+        def _():
+            wait(count)
+
+    def scatter_wait(src, ss, rs, base, count):
+        but_own(base, count, lambda n: several(src, ss, rs, n).wait_send())
+
+    def answer_wait(e_dst, es, er, base, count):
+        but_own(base, count, lambda n: several(e_dst, es, er, n).wait_recv())
+
+    def owner_wait(dst, ss, rs):
+        several(dst, ss, rs, n_seq - 1).wait_recv()
+
+    def owner_scan(dst, ss, rs, e_src, e_dst, es, er, base, backward):
         @pl.when(owns(base, units))
         def _():
-            owner_wait(src, dst, ss, rs)
+            owner_wait(dst, ss, rs)
             u = seq - base
             fade = avec[u]
 
@@ -158,37 +176,22 @@
 
             lax.fori_loop(0, n_seq, step, jnp.zeros((8, B), F32))
             e_dst[u] = e_src[seq]
-
-            @pl.loop(1, n_seq)
-            def _(d):
-                other = lax.rem(seq + d, n_seq)
-                remote(e_src.at[other], e_dst.at[u], es.at[other], er.at[u], "seq", other).start()
-
-    def owner_sends_wait(e_src, e_dst, es, er, base, count, one):
-        @pl.when(owns(base, count))
-        def _():
-            u = seq - base
-
-            @pl.loop(1, n_seq)
-            def _(d):
-                other = lax.rem(seq + d, n_seq)
-                src = e_src.at[0] if one else e_src.at[other]
-                remote(src, e_dst.at[u], es.at[other], er.at[u], "seq", other).wait_send()
-
-    eye_modes = lax.broadcasted_iota(jnp.int32, (GS, GS), 0) == lax.broadcasted_iota(jnp.int32, (GS, GS), 1)
+            answer(e_src, e_dst, es, er, u, False)
+
+    group_lane = lax.broadcasted_iota(jnp.int32, decay.shape, 1)
+    for fetch in fetches[2:6]:
+        fetch.wait()
     time = lane.astype(F32)
 
     @pl.loop(0, nt)
     def _(k):
-        def column(ref):
-            parts = []
-            for g in range(GT):
-                values = ref[pl.ds(k * GT + g, 1), :]
-                parts.append(jnp.sum(jnp.where(eye_modes, values, 0.0), axis=1, keepdims=True))
-            return jnp.concatenate(parts, axis=0)
-
-        rate = column(decay)
-        weight = column(resid) * jnp.sqrt(2.0 * rate)
+        def column(values):
+            return jnp.concatenate([
+                jnp.sum(jnp.where(group_lane == k * GT + g, values, 0.0), axis=1, keepdims=True) for g in range(GT)
+            ], axis=0)
+
+        rate = column(decay[...])
+        weight = column(resid[...]) * jnp.sqrt(2.0 * rate)
         fading = jnp.exp(-rate * time)
         hi, lo = split(fading)
         winb[k, 0:B, :] = hi
@@ -214,6 +217,8 @@
 
     scatter(bs_src, bs_dst, bs_s, bs_r, base_b, units)
 
+    for fetch in fetches[6:]:
+        fetch.wait()
     reflect = jnp.where(row == ((B - lane) & (B - 1)), 1.0, 0.0)
     taps[0] = filt[...].astype(BF16).astype(F32)
     for which in range(2):
@@ -235,7 +240,7 @@
     build(rtaps, 0, lane <= row, tmf)
     build(taps, 1, lane >= row, tlb)
 
-    owner_scan(bs_src, bs_dst, bs_s, bs_r, be_src, be_dst, be_s, be_r, base_b, True)
+    owner_scan(bs_dst, bs_s, bs_r, be_src, be_dst, be_s, be_r, base_b, True)
 
     def carried(wout, e_dst, k):
         state = jnp.concatenate([e_dst[2 * k], e_dst[2 * k + 1]], axis=0)
@@ -261,7 +266,7 @@
 
     squares = lax.fori_loop(0, nt, mr_step, squares)
 
-    answer_wait(be_src, be_dst, be_s, be_r, base_b, units)
+    answer_wait(be_dst, be_s, be_r, base_b, units)
 
     def li_step(k, cross):
         grad = gml[k] + carried(woutb, be_dst, k)
@@ -282,7 +287,7 @@
 
     def psum_copy(d):
         other = lax.rem(chan + d, n_chan)
-        return remote(pbuf.at[chan], pbuf.at[chan], p_s.at[other], p_r.at[chan], "chan", other)
+        return remote(pbuf.at[chan], pbuf.at[chan], p_s, p_r, "chan", other)
 
     @pl.loop(1, n_chan)
     def _(d):
@@ -291,10 +296,9 @@
     build(taps, 0, lane >= row, tmb)
     build(rtaps, 1, lane <= row, tlf)
 
-    @pl.loop(1, n_chan)
-    def _(d):
-        other = lax.rem(chan + d, n_chan)
-        remote(pbuf.at[other], pbuf.at[other], p_s.at[other], p_r.at[other], "chan", other).wait_recv()
+    psum_all = remote(pbuf.at[pl.ds(0, n_chan - 1)], pbuf.at[pl.ds(0, n_chan - 1)], p_s, p_r, "chan",
+                      lax.rem(chan + 1, n_chan))
+    psum_all.wait_recv()
 
     sums = pbuf[0]
     for c in range(1, n_chan):
@@ -342,10 +346,11 @@
         for g in range(GT):
             rows = gram[g * B:(g + 1) * B]
             cyclic = jnp.where(lane <= row, rows[:, 0:B], rows[:, B:2 * B])
-            acc = cyclic[B - 8:B]
-            for b in range(B // 8 - 2, -1, -1):
-                acc = pltpu.roll(acc, B - 8, axis=1) + cyclic[8 * b:8 * b + 8]
-            sums.append(acc)
+            half = B // 2
+            while half >= 8:
+                cyclic = cyclic[0:half] + pltpu.roll(cyclic[half:2 * half], B - half, axis=1)
+                half //= 2
+            sums.append(cyclic)
         acc = jnp.concatenate(sums, axis=0)
         for bit in range(3):
             acc = jnp.where(((row64 >> bit) & 1) == 1, pltpu.roll(acc, B - (1 << bit), axis=1), acc)
@@ -359,7 +364,7 @@
 
     scatter(r_src, r_dst, r_s, r_r, base_r, nt + 1)
 
-    owner_scan(fs_src, fs_dst, fs_s, fs_r, fe_src, fe_dst, fe_s, fe_r, base_f, False)
+    owner_scan(fs_dst, fs_s, fs_r, fe_src, fe_dst, fe_s, fe_r, base_f, False)
 
     @pl.loop(0, nt)
     def _(k):
@@ -367,18 +372,14 @@
 
     @pl.when(owns(base_r, nt + 1))
     def _():
-        owner_wait(r_src, r_dst, r_s, r_r)
+        owner_wait(r_dst, r_s, r_r)
         u = seq - base_r
         result = lax.fori_loop(1, n_seq, lambda q, acc: acc + r_dst[q], r_dst[0]) * scale
         a_src[0] = result
         a_dst[u] = result
-
-        @pl.loop(1, n_seq)
-        def _(d):
-            other = lax.rem(seq + d, n_seq)
-            remote(a_src.at[0], a_dst.at[u], a_s.at[other], a_r.at[u], "seq", other).start()
-
-    answer_wait(fe_src, fe_dst, fe_s, fe_r, base_f, units)
+        answer(a_src, a_dst, a_s, a_r, u, True)
+
+    answer_wait(fe_dst, fe_s, fe_r, base_f, units)
 
     @pl.loop(0, nt)
     def _(k):
@@ -396,33 +397,43 @@
         g_kmr[:, cols(k)] = (grad * tile(v_mr, k)).astype(BF16)
         g_vmr[:, cols(k)] = (grad * tile(k_mr, k)).astype(BF16)
 
-    answer_wait(a_src, a_dst, a_s, a_r, base_r, nt + 1)
+    answer_wait(a_dst, a_s, a_r, base_r, nt + 1)
     for k in range(nt):
         g_filt[k * 8:(k + 1) * 8, :] = a_dst[k]
     g_gain[...] = a_dst[nt, 0:nt, :]
 
     @pl.when(seq < n_seq - 1)
     def _():
-        @pl.loop(0, nt)
-        def _(k):
-            halo_f(k).wait_send()
+        remote(ext.at[:, pl.ds(0, B)], ext.at[:, pl.ds(B, B)], hf_s, hf_r.at[0], "seq", lax.rem(seq + 1, n_seq)).wait_send()
 
     @pl.when(seq > 0)
     def _():
-        @pl.loop(0, nt)
-        def _(k):
-            halo_b(k).wait_send()
-
-    scatter_wait(bs_src, bs_dst, bs_s, bs_r, base_b, units)
-    scatter_wait(fs_src, fs_dst, fs_s, fs_r, base_f, units)
-    scatter_wait(r_src, r_dst, r_s, r_r, base_r, nt + 1)
-    owner_sends_wait(be_src, be_dst, be_s, be_r, base_b, units, False)
-    owner_sends_wait(fe_src, fe_dst, fe_s, fe_r, base_f, units, False)
-    owner_sends_wait(a_src, a_dst, a_s, a_r, base_r, nt + 1, True)
-
-    @pl.loop(1, n_chan)
-    def _(d):
-        psum_copy(d).wait_send()
+        remote(bext.at[:, pl.ds(0, B)], bext.at[:, pl.ds(B, B)], hb_s, hb_r.at[0], "seq",
+               lax.rem(seq + n_seq - 1, n_seq)).wait_send()
+
+    scatter_wait(bs_src, bs_s, bs_r, base_b, units)
+    scatter_wait(fs_src, fs_s, fs_r, base_f, units)
+    scatter_wait(r_src, r_s, r_r, base_r, nt + 1)
+    for e_src, es, er, base in ((be_src, be_s, be_r, base_b), (fe_src, fe_s, fe_r, base_f)):
+        @pl.when(owns(base, units))
+        def _():
+            several(e_src, es, er, n_seq - 1).wait_send()
+
+    @pl.when(owns(base_r, nt + 1))
+    def _():
+        several(r_dst, a_s, a_r, n_seq - 1).wait_send()
+
+    psum_all.wait_send()
+
+
+def deliver(*refs):
+    count = len(refs) // 2
+    sem = refs[-1]
+    copies = [pltpu.make_async_copy(refs[i], refs[count + i], sem.at[i]) for i in range(count)]
+    for copy in copies:
+        copy.start()
+    for copy in copies:
+        copy.wait()
 
 
 def solution(mesh):
@@ -432,17 +443,24 @@
         rows, width = q_mr.shape
         nt = width // B
         units = 2 * nt
-        wide = jax.ShapeDtypeStruct((rows, width), BF16)
+        groups, taps_count = filt.shape
         vmem = pl.BlockSpec(memory_space=pltpu.VMEM)
+        hbm = pl.BlockSpec(memory_space=pltpu.HBM)
         dma = pltpu.SemaphoreType.DMA
+        one = dma(())
         state = lambda count: pltpu.VMEM((count, 8, B), F32)
         plane = lambda kind: pltpu.VMEM((nt, B, B), kind)
+        arguments = [
+            pltpu.with_memory_space_constraint(value, pltpu.HBM)
+            for value in (q_mr, k_mr, v_mr, q_li, k_li, cot, filt, gain.reshape(nt, B), decay.T, resid.T)
+        ]
+        shapes = [((rows, width), BF16)] * 6 + [((nt, B), F32), ((groups, taps_count), F32)]
         outs = pl.pallas_call(
             functools.partial(kernel, n_seq, n_chan, nt),
-            out_shape=[wide] * 6 + [jax.ShapeDtypeStruct((nt, B), F32), jax.ShapeDtypeStruct(filt.shape, F32)],
-            in_specs=[vmem] * 10,
+            out_shape=[jax.ShapeDtypeStruct(*shape) for shape in shapes],
+            in_specs=[hbm] * 10,
             out_specs=[vmem] * 8,
-            scratch_shapes=[
+            scratch_shapes=[pltpu.VMEM(value.shape, value.dtype) for value in arguments] + [
                 pltpu.VMEM((nt, 2 * B, B), BF16), pltpu.VMEM((nt, 2 * B, B), BF16),
                 pltpu.VMEM((nt, GT * B, 2 * B), BF16), pltpu.VMEM((nt, GT * B, 2 * B), BF16),
                 pltpu.VMEM((nt, GT * B, B), BF16), pltpu.VMEM((nt, GT * B, B), BF16),
@@ -453,16 +471,21 @@
                 state(units), state(n_seq), state(n_seq), state(units),
                 state(units), state(n_seq), state(n_seq), state(units),
                 state(n_chan), state(nt + 1), state(n_seq), state(1), state(nt + 1),
-                dma((nt,)), dma((nt,)), dma((nt,)), dma((nt,)),
-                dma((units,)), dma((n_seq,)), dma((n_seq,)), dma((units,)),
-                dma((units,)), dma((n_seq,)), dma((n_seq,)), dma((units,)),
-                dma((n_chan,)), dma((n_chan,)),
-                dma((nt + 1,)), dma((n_seq,)), dma((n_seq,)), dma((nt + 1,)),
+                dma((10,)), one, dma((nt,)), one, dma((nt,)),
+                one, one, one, one, one, one, one, one, one, one, one, one, one, one,
             ],
             compiler_params=pltpu.CompilerParams(
-                collective_id=0, has_side_effects=True, vmem_limit_bytes=48 * 1024 * 1024
+                collective_id=0, has_side_effects=True, vmem_limit_bytes=40 * 1024 * 1024
             ),
-        )(q_mr, k_mr, v_mr, q_li, k_li, cot, filt, gain.reshape(nt, B), decay, resid)
+        )(*arguments)
+        outs = pl.pallas_call(
+            deliver,
+            out_shape=[jax.ShapeDtypeStruct(*shape) for shape in shapes],
+            in_specs=[vmem] * 8,
+            out_specs=[hbm] * 8,
+            scratch_shapes=[dma((8,))],
+            compiler_params=pltpu.CompilerParams(vmem_limit_bytes=1024 * 1024),
+        )(*outs)
         return (*outs[:6], outs[6].reshape(width), outs[7])
 
     wide, by_group, by_chan = P("seq", "chan"), P("chan", None), P("chan")

time: 77.9 us -> 57.1 us (0.73)
  local copies, waits for them, and re-layouts: 12.6 us -> 0 us
  Pallas kernels: 63.9 us -> 56.3 us
    unnamed x28 -> x0, local copies, waits for them, and re-layouts: 12.6 us -> none
    pallas_call x1 -> x2, Pallas kernels: 63.9 us -> 56.3 us  [the longest x1 55.1 us: on_device(): pl.pallas_call(functools.partial(kernel, n_seq, n_chan, nt), out_shape=[j...]
where the time goes in v2:
time: 57.1 us; the launch traced here: 57 us
  Pallas kernels  56.3 us (99%)
  between operations  0.64 us (1%)
    pallas_call x1, Pallas kernels, on_device(): pl.pallas_call(functools.partial(kernel, n_seq, n_chan, nt), out_shape=[j...  55.1 us
    pallas_call x1, Pallas kernels, on_device(): pl.pallas_call(deliver, out_shape=[jax.ShapeDtypeStruct(*shape) for shape...  1.21 us

profile of v2, /device:TPU:32, one launch (start us, length us, event | category | flops | bytes accessed | tf_op | source)
XLA Modules:
  0.0 57.0 jit_solution(14516171682474409685)
XLA Ops:
  0.6 55.1 %shard_map.161 = (bf16[128,1024]{1,0:T(8,128)(2,1)S(1)}, bf16[128,1024]{1,0:T(8,128)(2,1)S(1)}, bf16[128,1024]{1,0:T(8,128)(2,1)S(1)}, bf16[128,1024]{1,0:T(8,12...) custom-call(bf16[128,1024]{1,0:T(8,128)(2,1)} %q_mr_in.1, ...), custom_call_target="tpu_custom_call" | custom-call | tf_op jit(solution)/shard_map/pallas_call | solution.py:458
  55.7 1.2 %shard_map.162 = (bf16[128,1024]{1,0:T(8,128)(2,1)}, bf16[128,1024]{1,0:T(8,128)(2,1)}, bf16[128,1024]{1,0:T(8,128)(2,1)}, bf16[128,1024]{1,0:T(8,128)(2,1)}, bf...) custom-call(bf16[128,1024]{1,0:T(8,128)(2,1)S(1)} %get-tuple-element.24.refs_0_, ...), custom_call_target="tpu_custom_call" | custom-call | tf_op jit(solution)/shard_map/pallas_call | solution.py:481

commit v3 on v2

v3 whole, which is shorter than its diff:
```python
import functools

import jax
import jax.numpy as jnp
from jax import lax
from jax.experimental import pallas as pl
from jax.experimental.pallas import tpu as pltpu
from jax.sharding import PartitionSpec as P

MESH = pl.DeviceIdType.MESH
F32 = jnp.float32
BF16 = jnp.bfloat16
B = 128
GS = 16
GT = B // GS
W = B + GS


def dot(a, b):
    return jnp.dot(a, b, preferred_element_type=F32)


def split(x):
    hi = x.astype(BF16)
    return hi, (x - hi.astype(F32)).astype(BF16)


def kernel(
    n_seq, n_chan, nt,
    q_mr_in, k_mr_in, v_mr_in, q_li_in, k_li_in, cot_in, filt_in, gain_in, decay_in, resid_in,
    out_li, g_qmr, g_kmr, g_vmr, g_qli, g_kli, g_gain, g_filt,
    q_mr, k_mr, v_mr, q_li, k_li, cot, filt, gain, decay, resid,
    ext, bext, tmf, tmb, tlf, tlb, conv, outm, gml, bli, xli, cli,
    winf, woutf, woutb, taps, rtaps, avec,
    bs_src, bs_dst, be_src, be_dst, fs_src, fs_dst, fe_src, fe_dst,
    pbuf, cbuf, r_src, r_dst, a_src, a_dst,
    in_sem, hf_s, hf_r, hb_s, hb_r, bs_s, bs_r, be_s, be_r, fs_s, fs_r, fe_s, fe_r,
    p_s, p_r, c_s, c_r, r_s, r_r, a_s, a_r,
):
    seq = lax.axis_index("seq")
    chan = lax.axis_index("chan")
    units = 2 * nt
    total = float(n_chan * nt * B)
    scale = float(n_seq * B) ** -0.5
    stride = n_seq // units
    owners_b = (0, stride, units)
    owners_f = (n_seq - 1 - stride * (units - 1), stride, units)
    owners_r = (0, n_seq // (nt + 1), nt + 1)

    lane = lax.broadcasted_iota(jnp.int32, (B, B), 1)
    row = lax.broadcasted_iota(jnp.int32, (B, B), 0)
    lane_group = lane >> 4
    diag_groups = (row >> 4) == lane_group
    eye = row == lane

    def cols(k):
        return pl.ds(pl.multiple_of(k * B, B), B)

    def tile(ref, k):
        return ref[:, cols(k)].astype(F32)

    lane_s = lax.broadcasted_iota(jnp.int32, (GS, B), 1)
    row_s = lax.broadcasted_iota(jnp.int32, (GS, B), 0)
    group_s = lane_s >> 4

    def windows(ref, k):
        return jnp.concatenate([ref[k, a * GS:a * GS + W, :] for a in range(GT)], axis=1)

    def banded(bands, ref, k):
        full = dot(bands[k], windows(ref, k))
        blocks = []
        for a in range(GT):
            part = full[:, a * B:(a + 1) * B]
            out = part[0:GS]
            for g in range(1, GT):
                out = jnp.where(group_s == g, part[g * GS:(g + 1) * GS], out)
            blocks.append(out)
        return jnp.concatenate(blocks, axis=0)

    def squeeze(full):
        return jnp.sum(jnp.where(diag_groups, full, 0.0).reshape(GT, GS, B), axis=0)

    def remote(src, dst, ss, rs, axis, target):
        return pltpu.make_async_remote_copy(
            src_ref=src, dst_ref=dst, send_sem=ss, recv_sem=rs,
            device_id={axis: target}, device_id_type=MESH,
        )

    fetches = [
        pltpu.make_async_copy(src, dst, in_sem.at[i])
        for i, (src, dst) in enumerate((
            (decay_in, decay), (cot_in, cot), (q_li_in, q_li), (k_mr_in, k_mr), (v_mr_in, v_mr),
            (resid_in, resid), (filt_in, filt), (gain_in, gain), (q_mr_in, q_mr), (k_li_in, k_li)))
    ]
    for fetch in fetches:
        fetch.start()

    barrier = pltpu.get_barrier_semaphore()

    @pl.loop(1, n_seq)
    def _(d):
        pl.semaphore_signal(barrier, inc=1, device_id={"seq": lax.rem(seq + d, n_seq)}, device_id_type=MESH)

    @pl.loop(1, n_chan)
    def _(d):
        pl.semaphore_signal(barrier, inc=1, device_id={"chan": lax.rem(chan + d, n_chan)}, device_id_type=MESH)

    time = lane.astype(F32)
    group_lane = lax.broadcasted_iota(jnp.int32, decay.shape, 1)

    def column(values, k):
        return jnp.concatenate([
            jnp.sum(jnp.where(group_lane == k * GT + g, values, 0.0), axis=1, keepdims=True) for g in range(GT)
        ], axis=0)

    for fetch in fetches[0:3]:
        fetch.wait()

    @pl.loop(0, nt, unroll=True)
    def _(k):
        hi, lo = split(jnp.exp(-column(decay[...], k) * time))
        back = (tile(cot, k) * tile(q_li, k)).astype(BF16)
        bli[k, 0:B, :] = back
        bli[k, B:2 * B, :] = jnp.zeros((B, B), BF16)
        xli[k, 0:B, :] = jnp.zeros((B, B), BF16)
        states = squeeze(dot(hi, back) + dot(lo, back))
        bs_src[2 * k] = states[0:8]
        bs_src[2 * k + 1] = states[8:16]

    pl.semaphore_wait(barrier, n_seq - 1 + n_chan - 1)

    def owns(owners):
        base, step, count = owners
        place = seq - base
        return jnp.logical_and(jnp.logical_and(place >= 0, place < step * count), lax.rem(place, step) == 0)

    def unit(owners):
        return lax.div(seq - owners[0], owners[1])

    def send_unit(src, dst, ss, rs, owners, u):
        owner = owners[0] + owners[1] * u

        @pl.when(seq != owner)
        def _():
            remote(src.at[u], dst.at[seq], ss, rs, "seq", owner).start()

        @pl.when(seq == owner)
        def _():
            dst[seq] = src[u]

    def scatter(src, dst, ss, rs, owners):
        @pl.loop(0, owners[2])
        def _(i):
            send_unit(src, dst, ss, rs, owners, lax.rem(seq + i, owners[2]))

    def answer(e_src, e_dst, es, er, u, one):
        @pl.loop(1, n_seq)
        def _(d):
            other = lax.rem(seq + d, n_seq)
            remote(e_src.at[0] if one else e_src.at[other], e_dst.at[u], es, er, "seq", other).start()

    def several(ref, ss, rs, count):
        return remote(ref.at[pl.ds(0, count)], ref.at[pl.ds(0, count)], ss, rs, "seq", lax.rem(seq + 1, n_seq))

    def but_own(owners, wait):
        count = owners[2]

        @pl.when(owns(owners))
        def _():
            wait(count - 1)

        @pl.when(jnp.logical_not(owns(owners)))
        def _():
            wait(count)

    def scatter_wait(src, ss, rs, owners):
        but_own(owners, lambda n: several(src, ss, rs, n).wait_send())

    def answer_wait(e_dst, es, er, owners):
        but_own(owners, lambda n: several(e_dst, es, er, n).wait_recv())

    def owner_wait(dst, ss, rs):
        several(dst, ss, rs, n_seq - 1).wait_recv()

    def owner_scan(dst, ss, rs, e_src, e_dst, es, er, owners, backward):
        @pl.when(owns(owners))
        def _():
            owner_wait(dst, ss, rs)
            u = unit(owners)
            fade = avec[u]

            def step(i, state):
                q = n_seq - 1 - i if backward else i
                e_src[q] = state
                return fade * state + dst[q]

            lax.fori_loop(0, n_seq, step, jnp.zeros((8, B), F32))
            e_dst[u] = e_src[seq]
            answer(e_src, e_dst, es, er, u, False)

    scatter(bs_src, bs_dst, bs_s, bs_r, owners_b)

    for fetch in fetches[3:5]:
        fetch.wait()

    @pl.loop(0, nt, unroll=True)
    def _(k):
        ext[k, B:2 * B, :] = (tile(k_mr, k) * tile(v_mr, k)).astype(BF16)

    def halo_f(k):
        return remote(ext.at[k, pl.ds(B, B)], ext.at[k, pl.ds(0, B)], hf_s, hf_r.at[k], "seq", lax.rem(seq + 1, n_seq))

    def halo_b(k):
        return remote(bext.at[k, pl.ds(0, B)], bext.at[k, pl.ds(B, B)], hb_s, hb_r.at[k], "seq",
                      lax.rem(seq + n_seq - 1, n_seq))

    @pl.when(seq < n_seq - 1)
    def _():
        @pl.loop(0, nt, unroll=True)
        def _(k):
            halo_f(k).start()

    @pl.when(seq == 0)
    def _():
        @pl.loop(0, nt, unroll=True)
        def _(k):
            ext[k, 0:B, :] = jnp.zeros((B, B), BF16)

    @pl.when(seq == n_seq - 1)
    def _():
        @pl.loop(0, nt, unroll=True)
        def _(k):
            bext[k, B:2 * B, :] = jnp.zeros((B, B), BF16)

    for fetch in fetches[5:]:
        fetch.wait()

    @pl.loop(0, nt, unroll=True)
    def _(k):
        rate = column(decay[...], k)
        weight = column(resid[...], k) * jnp.sqrt(2.0 * rate)
        fading = jnp.exp(-rate * time)
        powers = squeeze(jnp.broadcast_to(jnp.exp(-rate * float(B)), (B, B)))
        avec[2 * k] = powers[0:8]
        avec[2 * k + 1] = powers[8:16]
        taps[1, pl.ds(pl.multiple_of(k * GT, GT), GT), :] = jnp.sum((weight * fading).reshape(GT, GS, B), axis=1)
        hi, lo = split(jnp.exp(-rate * (B - 1.0 - time)))
        winf[k, 0:B, :] = hi
        winf[k, B:2 * B, :] = lo
        hi, lo = split((weight * jnp.exp(-rate * (B - time))).T)
        woutb[k, :, 0:B] = hi
        woutb[k, :, B:2 * B] = lo
        hi, lo = split((weight * jnp.exp(-rate * (time + 1.0))).T)
        woutf[k, :, 0:B] = hi
        woutf[k, :, B:2 * B] = lo

    reflect = jnp.where(row == ((B - lane) & (B - 1)), 1.0, 0.0)
    taps[0] = filt[...].astype(BF16).astype(F32)
    for which in range(2):
        rtaps[which] = dot(taps[which].astype(BF16), reflect.astype(BF16))

    @pl.loop(0, nt, unroll=True)
    def _(k):
        for ref, which, keep, out in (
            (taps, 1, lane_s >= row_s, tlb), (rtaps, 0, lane_s > row_s, tmf),
            (taps, 0, lane_s >= row_s, tmb), (rtaps, 1, lane_s > row_s, tlf),
        ):
            for g in range(GT):
                line = jnp.broadcast_to(ref[which, pl.ds(k * GT + g, 1), :], (GS, B))
                matrix = pltpu.roll(line, 0, axis=1, stride=1, stride_axis=0)
                out[k, g * GS:(g + 1) * GS, 0:B] = jnp.where(keep, matrix, 0.0).astype(BF16)
                out[k, g * GS:(g + 1) * GS, B:W] = jnp.where(keep, 0.0, matrix)[:, 0:GS].astype(BF16)

    def carried(wout, e_dst, k):
        state = jnp.concatenate([e_dst[2 * k], e_dst[2 * k + 1]], axis=0)
        hi, lo = split(jnp.where(diag_groups, jnp.concatenate([state] * GT, axis=0), 0.0))
        return dot(wout[k], jnp.concatenate([hi, hi], axis=0)) + dot(wout[k, :, 0:B], lo)

    @pl.loop(0, nt, unroll=True)
    def _(k):
        gml[k] = banded(tlb, bli, k)

    owner_scan(bs_dst, bs_s, bs_r, be_src, be_dst, be_s, be_r, owners_b, True)

    squares = jnp.zeros((B, B), F32)

    def mr_step(k, squares):
        @pl.when(seq > 0)
        def _():
            halo_f(k).wait_recv()

        value = banded(tmf, ext, k)
        conv[k] = value
        gated = (tile(q_mr, k) * value).astype(BF16).astype(F32)
        outm[k] = gated
        return squares + gated * gated

    squares = lax.fori_loop(0, nt, mr_step, squares, unroll=True)

    def as_row(partial):
        column = jnp.sum(partial, axis=1, keepdims=True)
        return jnp.sum(jnp.where(eye, column, 0.0), axis=0, keepdims=True)

    def as_column(line):
        return jnp.sum(jnp.where(eye, line, 0.0), axis=1, keepdims=True)

    def all_of(buf, ss, rs):
        part = buf.at[pl.ds(0, n_chan - 1)]
        return remote(part, part, ss, rs, "chan", lax.rem(chan + 1, n_chan))

    def psum_start(buf, partial, ss, rs):
        buf[chan] = jnp.broadcast_to(as_row(partial), (8, B))

        @pl.loop(1, n_chan)
        def _(d):
            remote(buf.at[chan], buf.at[chan], ss, rs, "chan", lax.rem(chan + d, n_chan)).start()

    def psum_end(buf, ss, rs):
        all_of(buf, ss, rs).wait_recv()
        sums = buf[0]
        for c in range(1, n_chan):
            sums = sums + buf[c]
        return sums[0:1]

    psum_start(pbuf, squares, p_s, p_r)
    inv_row = lax.rsqrt(psum_end(pbuf, p_s, p_r) / total + 1e-06)
    inv = as_column(inv_row)

    @pl.loop(0, nt, unroll=True)
    def _(k):
        normed = outm[k] * inv * gain[pl.ds(k, 1), :]
        mixed = (tile(k_li, k) * normed).astype(BF16)
        xli[k, B:2 * B, :] = mixed
        both = dot(winf[k], mixed)
        states = squeeze(both[0:B] + both[B:2 * B])
        fs_src[2 * k] = states[0:8]
        fs_src[2 * k + 1] = states[8:16]

    scatter(fs_src, fs_dst, fs_s, fs_r, owners_f)

    answer_wait(be_dst, be_s, be_r, owners_b)

    def li_step(k, cross):
        grad = gml[k] + carried(woutb, be_dst, k)
        gml[k] = grad
        return cross + grad * tile(k_li, k) * outm[k] * gain[pl.ds(k, 1), :]

    cross = lax.fori_loop(0, nt, li_step, jnp.zeros((B, B), F32), unroll=True)
    psum_start(cbuf, cross, c_s, c_r)

    @pl.loop(0, nt, unroll=True)
    def _(k):
        grad, scaled = gml[k], outm[k] * inv
        g_kli[:, cols(k)] = (grad * (scaled * gain[pl.ds(k, 1), :])).astype(BF16)
        r_src[nt, pl.ds(k, 1), :] = jnp.sum(grad * tile(k_li, k) * scaled, axis=0, keepdims=True)
        cli[k] = banded(tlf, xli, k)

    if nt < 8:
        r_src[nt, nt:8, :] = jnp.zeros((8 - nt, B), F32)
    send_unit(r_src, r_dst, r_s, r_r, owners_r, nt)

    pull = as_column(inv_row * inv_row * inv_row * psum_end(cbuf, c_s, c_r) / total)

    @pl.loop(0, nt, unroll=True)
    def _(k):
        grad_out = inv * (gml[k] * tile(k_li, k) * gain[pl.ds(k, 1), :]) - outm[k] * pull
        bext[k, 0:B, :] = (grad_out * tile(q_mr, k)).astype(BF16)

        @pl.when(seq > 0)
        def _():
            halo_b(k).start()

        g_qmr[:, cols(k)] = (grad_out * conv[k]).astype(BF16)

    row64 = lax.broadcasted_iota(jnp.int32, (8 * GT, B), 0)

    @pl.loop(0, nt, unroll=True)
    def _(k):
        back = bext[k, 0:B, :]
        masked = jnp.concatenate([
            jnp.concatenate([
                jnp.where(group_s == g, back[a * GS:(a + 1) * GS], jnp.zeros((GS, B), BF16)) for a in range(GT)
            ], axis=1) for g in range(GT)
        ], axis=0)
        gram = lax.dot_general(masked, windows(ext, k), (((1,), (1,)), ((), ())), preferred_element_type=F32)
        wrapped = jnp.concatenate([gram[:, B:W], jnp.zeros((B, B - GS), F32)], axis=1)
        cyclic = jnp.where(lane <= (row & (GS - 1)), wrapped, gram[:, 0:B])
        sums = [
            cyclic[g * GS:g * GS + 8] + pltpu.roll(cyclic[g * GS + 8:(g + 1) * GS], B - 8, axis=1) for g in range(GT)
        ]
        acc = jnp.concatenate(sums, axis=0)
        for bit in range(3):
            acc = jnp.where(((row64 >> bit) & 1) == 1, pltpu.roll(acc, B - (1 << bit), axis=1), acc)
        diagonals = jnp.sum(acc.reshape(GT, 8, B), axis=1)
        hi = diagonals.astype(BF16)
        rest = diagonals - hi.astype(F32)
        mid, lo = split(rest)
        parts = dot(jnp.concatenate([hi.astype(F32), mid.astype(F32), lo.astype(F32)], axis=0).astype(BF16),
                    reflect.astype(BF16))
        r_src[k] = parts[0:8] + parts[8:16] + parts[16:24]
        send_unit(r_src, r_dst, r_s, r_r, owners_r, k)

    owner_scan(fs_dst, fs_s, fs_r, fe_src, fe_dst, fe_s, fe_r, owners_f, False)

    @pl.when(owns(owners_r))
    def _():
        owner_wait(r_dst, r_s, r_r)
        u = unit(owners_r)
        result = lax.fori_loop(1, n_seq, lambda q, acc: acc + r_dst[q], r_dst[0]) * scale
        a_src[0] = result
        a_dst[u] = result
        answer(a_src, a_dst, a_s, a_r, u, True)

    answer_wait(fe_dst, fe_s, fe_r, owners_f)

    @pl.loop(0, nt, unroll=True)
    def _(k):
        value = cli[k] + carried(woutf, fe_dst, k)
        out_li[:, cols(k)] = (tile(q_li, k) * value).astype(BF16)
        g_qli[:, cols(k)] = (tile(cot, k) * value).astype(BF16)

    @pl.loop(0, nt, unroll=True)
    def _(k):
        @pl.when(seq < n_seq - 1)
        def _():
            halo_b(k).wait_recv()

        grad = banded(tmb, bext, k)
        g_kmr[:, cols(k)] = (grad * tile(v_mr, k)).astype(BF16)
        g_vmr[:, cols(k)] = (grad * tile(k_mr, k)).astype(BF16)

    answer_wait(a_dst, a_s, a_r, owners_r)
    for k in range(nt):
        g_filt[k * 8:(k + 1) * 8, :] = a_dst[k]
    g_gain[...] = a_dst[nt, 0:nt, :]

    @pl.when(seq < n_seq - 1)
    def _():
        remote(ext.at[:, pl.ds(B, B)], ext.at[:, pl.ds(0, B)], hf_s, hf_r.at[0], "seq", lax.rem(seq + 1, n_seq)).wait_send()

    @pl.when(seq > 0)
    def _():
        remote(bext.at[:, pl.ds(0, B)], bext.at[:, pl.ds(B, B)], hb_s, hb_r.at[0], "seq",
               lax.rem(seq + n_seq - 1, n_seq)).wait_send()

    scatter_wait(bs_src, bs_s, bs_r, owners_b)
    scatter_wait(fs_src, fs_s, fs_r, owners_f)
    scatter_wait(r_src, r_s, r_r, owners_r)
    for e_src, es, er, owners in ((be_src, be_s, be_r, owners_b), (fe_src, fe_s, fe_r, owners_f)):
        @pl.when(owns(owners))
        def _():
            several(e_src, es, er, n_seq - 1).wait_send()

    @pl.when(owns(owners_r))
    def _():
        several(r_dst, a_s, a_r, n_seq - 1).wait_send()

    all_of(pbuf, p_s, p_r).wait_send()
    all_of(cbuf, c_s, c_r).wait_send()


def deliver(*refs):
    count = len(refs) // 2
    sem = refs[-1]
    copies = [pltpu.make_async_copy(refs[i], refs[count + i], sem.at[i]) for i in range(count)]
    for copy in copies:
        copy.start()
    for copy in copies:
        copy.wait()


def solution(mesh):
    n_seq, n_chan = mesh.shape["seq"], mesh.shape["chan"]

    def on_device(q_mr, k_mr, v_mr, q_li, k_li, cot, filt, gain, decay, resid):
        rows, width = q_mr.shape
        nt = width // B
        units = 2 * nt
        groups, taps_count = filt.shape
        vmem = pl.BlockSpec(memory_space=pltpu.VMEM)
        hbm = pl.BlockSpec(memory_space=pltpu.HBM)
        dma = pltpu.SemaphoreType.DMA
        one = dma(())
        state = lambda count: pltpu.VMEM((count, 8, B), F32)
        plane = lambda kind: pltpu.VMEM((nt, B, B), kind)
        arguments = [
            pltpu.with_memory_space_constraint(value, pltpu.HBM)
            for value in (q_mr, k_mr, v_mr, q_li, k_li, cot, filt, gain.reshape(nt, B), decay.T, resid.T)
        ]
        shapes = [((rows, width), BF16)] * 6 + [((nt, B), F32), ((groups, taps_count), F32)]
        outs = pl.pallas_call(
            functools.partial(kernel, n_seq, n_chan, nt),
            out_shape=[jax.ShapeDtypeStruct(*shape) for shape in shapes],
            in_specs=[hbm] * 10,
            out_specs=[vmem] * 8,
            scratch_shapes=[pltpu.VMEM(value.shape, value.dtype) for value in arguments] + [
                pltpu.VMEM((nt, 2 * B, B), BF16), pltpu.VMEM((nt, 2 * B, B), BF16),
                pltpu.VMEM((nt, B, W), BF16), pltpu.VMEM((nt, B, W), BF16),
                pltpu.VMEM((nt, B, W), BF16), pltpu.VMEM((nt, B, W), BF16),
                plane(F32), plane(F32), plane(F32), pltpu.VMEM((nt, 2 * B, B), BF16), pltpu.VMEM((nt, 2 * B, B), BF16), plane(F32),
                pltpu.VMEM((nt, 2 * B, B), BF16),
                pltpu.VMEM((nt, B, 2 * B), BF16), pltpu.VMEM((nt, B, 2 * B), BF16),
                pltpu.VMEM((2, nt * GT, B), F32), pltpu.VMEM((2, nt * GT, B), F32), state(units),
                state(units), state(n_seq), state(n_seq), state(units),
                state(units), state(n_seq), state(n_seq), state(units),
                state(n_chan), state(n_chan), state(nt + 1), state(n_seq), state(1), state(nt + 1),
                dma((10,)), one, dma((nt,)), one, dma((nt,)),
                one, one, one, one, one, one, one, one, one, one, one, one, one, one, one, one,
            ],
            compiler_params=pltpu.CompilerParams(
                collective_id=0, has_side_effects=True, vmem_limit_bytes=40 * 1024 * 1024
            ),
        )(*arguments)
        outs = pl.pallas_call(
            deliver,
            out_shape=[jax.ShapeDtypeStruct(*shape) for shape in shapes],
            in_specs=[vmem] * 8,
            out_specs=[hbm] * 8,
            scratch_shapes=[dma((8,))],
            compiler_params=pltpu.CompilerParams(vmem_limit_bytes=1024 * 1024),
        )(*outs)
        return (*outs[:6], outs[6].reshape(width), outs[7])

    wide, by_group, by_chan = P("seq", "chan"), P("chan", None), P("chan")
    return jax.shard_map(
        on_device, mesh=mesh,
        in_specs=(wide,) * 6 + (by_group, by_chan, by_group, by_group),
        out_specs=(wide,) * 6 + (by_chan, by_group),
        check_vma=False,
    )
```

time: 57.1 us -> 48.6 us (0.85)
  Pallas kernels: 56.3 us -> 47.8 us
    pallas_call x1, Pallas kernels: 55.1 us -> 46.6 us  [on_device(): pl.pallas_call(functools.partial(kernel, n_seq, n_chan, nt), out_shape=[j...]
where the time goes in v3:
time: 48.6 us; the launch traced here: 48.4 us
  Pallas kernels  47.8 us (98%)
  between operations  0.64 us (1%)
    pallas_call x1, Pallas kernels, on_device(): pl.pallas_call(functools.partial(kernel, n_seq, n_chan, nt), out_shape=[j...  46.6 us
    pallas_call x1, Pallas kernels, on_device(): pl.pallas_call(deliver, out_shape=[jax.ShapeDtypeStruct(*shape) for shape...  1.21 us

profile of v3, /device:TPU:32, one launch (start us, length us, event | category | flops | bytes accessed | tf_op | source)
XLA Modules:
  0.0 48.4 jit_solution(3247722058737542160)
XLA Ops:
  0.6 46.6 %shard_map.161 = (bf16[128,1024]{1,0:T(8,128)(2,1)S(1)}, bf16[128,1024]{1,0:T(8,128)(2,1)S(1)}, bf16[128,1024]{1,0:T(8,128)(2,1)S(1)}, bf16[128,1024]{1,0:T(8,12...) custom-call(bf16[128,1024]{1,0:T(8,128)(2,1)} %q_mr_in.1, ...), custom_call_target="tpu_custom_call" | custom-call | tf_op jit(solution)/shard_map/pallas_call | solution.py:491
  47.2 1.2 %shard_map.162 = (bf16[128,1024]{1,0:T(8,128)(2,1)}, bf16[128,1024]{1,0:T(8,128)(2,1)}, bf16[128,1024]{1,0:T(8,128)(2,1)}, bf16[128,1024]{1,0:T(8,128)(2,1)}, bf...) custom-call(bf16[128,1024]{1,0:T(8,128)(2,1)S(1)} %get-tuple-element.24.refs_0_, ...), custom_call_target="tpu_custom_call" | custom-call | tf_op jit(solution)/shard_map/pallas_call | solution.py:514

commit v4 on v3

--- a/solution.py
+++ b/solution.py
@@ -45,7 +45,23 @@
     stride = n_seq // units
     owners_b = (0, stride, units)
     owners_f = (n_seq - 1 - stride * (units - 1), stride, units)
-    owners_r = (0, n_seq // (nt + 1), nt + 1)
+    sums_r = nt // 2 + 1
+    owners_r = (0, n_seq // sums_r, sums_r)
+    nz = 8 if n_seq % 8 == 0 else n_seq
+    ny = n_seq // nz
+    my_y, my_z = lax.div(seq, nz), lax.rem(seq, nz)
+
+    def ring_order(i, n):
+        return lax.rem(n // 2 + n + lax.div(i + 1, 2) * (1 - 2 * lax.rem(i, 2)), n)
+
+    def far_first(i):
+        dy, dz = ring_order(lax.rem(i, ny), ny), ring_order(lax.div(i, ny), nz)
+        return lax.rem(my_y + dy, ny) * nz + lax.rem(my_z + dz, nz)
+
+    def far_first_unit(i, count):
+        wide = count // ny
+        dy, dz = ring_order(lax.rem(i, ny), ny), ring_order(lax.div(i, ny), wide)
+        return lax.rem(my_y + dy, ny) * wide + lax.rem(lax.div(my_z * wide, nz) + dz, wide)
 
     lane = lax.broadcasted_iota(jnp.int32, (B, B), 1)
     row = lax.broadcasted_iota(jnp.int32, (B, B), 0)
@@ -86,6 +102,16 @@
             device_id={axis: target}, device_id_type=MESH,
         )
 
+    barrier = pltpu.get_barrier_semaphore()
+
+    @pl.loop(0, n_seq - 1)
+    def _(i):
+        pl.semaphore_signal(barrier, inc=1, device_id={"seq": far_first(i)}, device_id_type=MESH)
+
+    @pl.loop(1, n_chan)
+    def _(d):
+        pl.semaphore_signal(barrier, inc=1, device_id={"chan": lax.rem(chan + d, n_chan)}, device_id_type=MESH)
+
     fetches = [
         pltpu.make_async_copy(src, dst, in_sem.at[i])
         for i, (src, dst) in enumerate((
@@ -95,16 +121,6 @@
     for fetch in fetches:
         fetch.start()
 
-    barrier = pltpu.get_barrier_semaphore()
-
-    @pl.loop(1, n_seq)
-    def _(d):
-        pl.semaphore_signal(barrier, inc=1, device_id={"seq": lax.rem(seq + d, n_seq)}, device_id_type=MESH)
-
-    @pl.loop(1, n_chan)
-    def _(d):
-        pl.semaphore_signal(barrier, inc=1, device_id={"chan": lax.rem(chan + d, n_chan)}, device_id_type=MESH)
-
     time = lane.astype(F32)
     group_lane = lax.broadcasted_iota(jnp.int32, decay.shape, 1)
 
@@ -151,12 +167,12 @@
     def scatter(src, dst, ss, rs, owners):
         @pl.loop(0, owners[2])
         def _(i):
-            send_unit(src, dst, ss, rs, owners, lax.rem(seq + i, owners[2]))
+            send_unit(src, dst, ss, rs, owners, far_first_unit(i, owners[2]))
 
     def answer(e_src, e_dst, es, er, u, one):
-        @pl.loop(1, n_seq)
-        def _(d):
-            other = lax.rem(seq + d, n_seq)
+        @pl.loop(0, n_seq - 1)
+        def _(i):
+            other = far_first(i)
             remote(e_src.at[0] if one else e_src.at[other], e_dst.at[u], es, er, "seq", other).start()
 
     def several(ref, ss, rs, count):
@@ -194,7 +210,7 @@
                 e_src[q] = state
                 return fade * state + dst[q]
 
-            lax.fori_loop(0, n_seq, step, jnp.zeros((8, B), F32))
+            lax.fori_loop(0, n_seq, step, jnp.zeros((8, B), F32), unroll=8 if n_seq % 8 == 0 else 1)
             e_dst[u] = e_src[seq]
             answer(e_src, e_dst, es, er, u, False)
 
@@ -305,22 +321,23 @@
         return jnp.sum(jnp.where(eye, line, 0.0), axis=1, keepdims=True)
 
     def all_of(buf, ss, rs):
-        part = buf.at[pl.ds(0, n_chan - 1)]
+        part = buf.at[pl.ds(0, n_chan - 1), pl.ds(0, 1)]
         return remote(part, part, ss, rs, "chan", lax.rem(chan + 1, n_chan))
 
     def psum_start(buf, partial, ss, rs):
-        buf[chan] = jnp.broadcast_to(as_row(partial), (8, B))
+        buf[chan, 0:1, :] = as_row(partial)
+        mine = buf.at[chan, pl.ds(0, 1)]
 
         @pl.loop(1, n_chan)
         def _(d):
-            remote(buf.at[chan], buf.at[chan], ss, rs, "chan", lax.rem(chan + d, n_chan)).start()
+            remote(mine, mine, ss, rs, "chan", lax.rem(chan + d, n_chan)).start()
 
     def psum_end(buf, ss, rs):
         all_of(buf, ss, rs).wait_recv()
-        sums = buf[0]
+        sums = buf[0, 0:1, :]
         for c in range(1, n_chan):
-            sums = sums + buf[c]
-        return sums[0:1]
+            sums = sums + buf[c, 0:1, :]
+        return sums
 
     psum_start(pbuf, squares, p_s, p_r)
     inv_row = lax.rsqrt(psum_end(pbuf, p_s, p_r) / total + 1e-06)
@@ -348,16 +365,15 @@
     cross = lax.fori_loop(0, nt, li_step, jnp.zeros((B, B), F32), unroll=True)
     psum_start(cbuf, cross, c_s, c_r)
 
-    @pl.loop(0, nt, unroll=True)
-    def _(k):
+    gains = []
+    for k in range(nt):
         grad, scaled = gml[k], outm[k] * inv
         g_kli[:, cols(k)] = (grad * (scaled * gain[pl.ds(k, 1), :])).astype(BF16)
-        r_src[nt, pl.ds(k, 1), :] = jnp.sum(grad * tile(k_li, k) * scaled, axis=0, keepdims=True)
+        gains.append(jnp.sum(grad * tile(k_li, k) * scaled, axis=0, keepdims=True))
         cli[k] = banded(tlf, xli, k)
-
-    if nt < 8:
-        r_src[nt, nt:8, :] = jnp.zeros((8 - nt, B), F32)
-    send_unit(r_src, r_dst, r_s, r_r, owners_r, nt)
+    gains.append(jnp.zeros((16 - nt, B), F32))
+    r_src[nt // 2] = jnp.concatenate(gains, axis=0).astype(BF16)
+    send_unit(r_src, r_dst, r_s, r_r, owners_r, nt // 2)
 
     pull = as_column(inv_row * inv_row * inv_row * psum_end(cbuf, c_s, c_r) / total)
 
@@ -366,16 +382,12 @@
         grad_out = inv * (gml[k] * tile(k_li, k) * gain[pl.ds(k, 1), :]) - outm[k] * pull
         bext[k, 0:B, :] = (grad_out * tile(q_mr, k)).astype(BF16)
 
-        @pl.when(seq > 0)
-        def _():
-            halo_b(k).start()
-
         g_qmr[:, cols(k)] = (grad_out * conv[k]).astype(BF16)
 
     row64 = lax.broadcasted_iota(jnp.int32, (8 * GT, B), 0)
 
-    @pl.loop(0, nt, unroll=True)
-    def _(k):
+    halves = []
+    for k in range(nt):
         back = bext[k, 0:B, :]
         masked = jnp.concatenate([
             jnp.concatenate([
@@ -391,22 +403,24 @@
         acc = jnp.concatenate(sums, axis=0)
         for bit in range(3):
             acc = jnp.where(((row64 >> bit) & 1) == 1, pltpu.roll(acc, B - (1 << bit), axis=1), acc)
-        diagonals = jnp.sum(acc.reshape(GT, 8, B), axis=1)
-        hi = diagonals.astype(BF16)
-        rest = diagonals - hi.astype(F32)
-        mid, lo = split(rest)
-        parts = dot(jnp.concatenate([hi.astype(F32), mid.astype(F32), lo.astype(F32)], axis=0).astype(BF16),
-                    reflect.astype(BF16))
-        r_src[k] = parts[0:8] + parts[8:16] + parts[16:24]
-        send_unit(r_src, r_dst, r_s, r_r, owners_r, k)
+        halves.append(jnp.sum(acc.reshape(GT, 8, B), axis=1))
+        if k % 2:
+            r_src[k // 2] = jnp.concatenate(halves[-2:], axis=0).astype(BF16)
+            send_unit(r_src, r_dst, r_s, r_r, owners_r, k // 2)
 
     owner_scan(fs_dst, fs_s, fs_r, fe_src, fe_dst, fe_s, fe_r, owners_f, False)
+
+    @pl.when(seq > 0)
+    def _():
+        @pl.loop(0, nt)
+        def _(k):
+            halo_b(k).start()
 
     @pl.when(owns(owners_r))
     def _():
         owner_wait(r_dst, r_s, r_r)
         u = unit(owners_r)
-        result = lax.fori_loop(1, n_seq, lambda q, acc: acc + r_dst[q], r_dst[0]) * scale
+        result = jnp.sum(r_dst[...].astype(F32), axis=0).astype(BF16)
         a_src[0] = result
         a_dst[u] = result
         answer(a_src, a_dst, a_s, a_r, u, True)
@@ -430,9 +444,9 @@
         g_vmr[:, cols(k)] = (grad * tile(k_mr, k)).astype(BF16)
 
     answer_wait(a_dst, a_s, a_r, owners_r)
-    for k in range(nt):
-        g_filt[k * 8:(k + 1) * 8, :] = a_dst[k]
-    g_gain[...] = a_dst[nt, 0:nt, :]
+    sums = jnp.concatenate([a_dst[u] for u in range(nt // 2)], axis=0)
+    g_filt[...] = dot(sums, reflect.astype(BF16)) * scale
+    g_gain[...] = a_dst[nt // 2].astype(F32)[0:nt] * scale
 
     @pl.when(seq < n_seq - 1)
     def _():
@@ -482,6 +496,7 @@
         dma = pltpu.SemaphoreType.DMA
         one = dma(())
         state = lambda count: pltpu.VMEM((count, 8, B), F32)
+        part = lambda count: pltpu.VMEM((count, 16, B), BF16)
         plane = lambda kind: pltpu.VMEM((nt, B, B), kind)
         arguments = [
             pltpu.with_memory_space_constraint(value, pltpu.HBM)
@@ -503,7 +518,7 @@
                 pltpu.VMEM((2, nt * GT, B), F32), pltpu.VMEM((2, nt * GT, B), F32), state(units),
                 state(units), state(n_seq), state(n_seq), state(units),
                 state(units), state(n_seq), state(n_seq), state(units),
-                state(n_chan), state(n_chan), state(nt + 1), state(n_seq), state(1), state(nt + 1),
+                state(n_chan), state(n_chan), part(nt // 2 + 1), part(n_seq), part(1), part(nt // 2 + 1),
                 dma((10,)), one, dma((nt,)), one, dma((nt,)),
                 one, one, one, one, one, one, one, one, one, one, one, one, one, one, one, one,
             ],

time: 48.6 us -> 44.8 us (0.922); the launches traced: 48.4 us -> 44.1 us
  Pallas kernels: 47.8 us -> 43.4 us
    pallas_call x1, Pallas kernels: 46.6 us -> 42.2 us  [on_device(): pl.pallas_call(functools.partial(kernel, n_seq, n_chan, nt), out_shape=[j...]
where the time goes in v4:
time: 44.8 us; the launch traced here: 44.1 us
  Pallas kernels  43.4 us (97%)
  between operations  0.64 us (1%)
    pallas_call x1, Pallas kernels, on_device(): pl.pallas_call(functools.partial(kernel, n_seq, n_chan, nt), out_shape=[j...  42.2 us
    pallas_call x1, Pallas kernels, on_device(): pl.pallas_call(deliver, out_shape=[jax.ShapeDtypeStruct(*shape) for shape...  1.21 us

profile of v4, /device:TPU:32, one launch (start us, length us, event | category | flops | bytes accessed | tf_op | source)
XLA Modules:
  0.0 44.1 jit_solution(16574160489824601606)
XLA Ops:
  0.6 42.2 %shard_map.161 = (bf16[128,1024]{1,0:T(8,128)(2,1)S(1)}, bf16[128,1024]{1,0:T(8,128)(2,1)S(1)}, bf16[128,1024]{1,0:T(8,128)(2,1)S(1)}, bf16[128,1024]{1,0:T(8,12...) custom-call(bf16[128,1024]{1,0:T(8,128)(2,1)} %q_mr_in.1, ...), custom_call_target="tpu_custom_call" | custom-call | tf_op jit(solution)/shard_map/pallas_call | solution.py:506
  42.8 1.2 %shard_map.162 = (bf16[128,1024]{1,0:T(8,128)(2,1)}, bf16[128,1024]{1,0:T(8,128)(2,1)}, bf16[128,1024]{1,0:T(8,128)(2,1)}, bf16[128,1024]{1,0:T(8,128)(2,1)}, bf...) custom-call(bf16[128,1024]{1,0:T(8,128)(2,1)S(1)} %get-tuple-element.24.refs_0_, ...), custom_call_target="tpu_custom_call" | custom-call | tf_op jit(solution)/shard_map/pallas_call | solution.py:529

commit v5 on v4

--- a/solution.py
+++ b/solution.py
@@ -143,6 +143,13 @@
         bs_src[2 * k] = states[0:8]
         bs_src[2 * k + 1] = states[8:16]
 
+    for fetch in fetches[3:5]:
+        fetch.wait()
+
+    @pl.loop(0, nt, unroll=True)
+    def _(k):
+        ext[k, B:2 * B, :] = (tile(k_mr, k) * tile(v_mr, k)).astype(BF16)
+
     pl.semaphore_wait(barrier, n_seq - 1 + n_chan - 1)
 
     def owns(owners):
@@ -215,13 +222,6 @@
             answer(e_src, e_dst, es, er, u, False)
 
     scatter(bs_src, bs_dst, bs_s, bs_r, owners_b)
-
-    for fetch in fetches[3:5]:
-        fetch.wait()
-
-    @pl.loop(0, nt, unroll=True)
-    def _(k):
-        ext[k, B:2 * B, :] = (tile(k_mr, k) * tile(v_mr, k)).astype(BF16)
 
     def halo_f(k):
         return remote(ext.at[k, pl.ds(B, B)], ext.at[k, pl.ds(0, B)], hf_s, hf_r.at[k], "seq", lax.rem(seq + 1, n_seq))
@@ -328,9 +328,9 @@
         buf[chan, 0:1, :] = as_row(partial)
         mine = buf.at[chan, pl.ds(0, 1)]
 
-        @pl.loop(1, n_chan)
-        def _(d):
-            remote(mine, mine, ss, rs, "chan", lax.rem(chan + d, n_chan)).start()
+        @pl.loop(0, n_chan - 1)
+        def _(i):
+            remote(mine, mine, ss, rs, "chan", lax.rem(chan + ring_order(i, n_chan), n_chan)).start()
 
     def psum_end(buf, ss, rs):
         all_of(buf, ss, rs).wait_recv()
@@ -340,6 +340,16 @@
         return sums
 
     psum_start(pbuf, squares, p_s, p_r)
+    answer_wait(be_dst, be_s, be_r, owners_b)
+
+    def li_step(k, cross):
+        grad = gml[k] + carried(woutb, be_dst, k)
+        gml[k] = grad
+        return cross + grad * tile(k_li, k) * outm[k] * gain[pl.ds(k, 1), :]
+
+    cross = lax.fori_loop(0, nt, li_step, jnp.zeros((B, B), F32), unroll=True)
+    psum_start(cbuf, cross, c_s, c_r)
+
     inv_row = lax.rsqrt(psum_end(pbuf, p_s, p_r) / total + 1e-06)
     inv = as_column(inv_row)
 
@@ -354,16 +364,6 @@
         fs_src[2 * k + 1] = states[8:16]
 
     scatter(fs_src, fs_dst, fs_s, fs_r, owners_f)
-
-    answer_wait(be_dst, be_s, be_r, owners_b)
-
-    def li_step(k, cross):
-        grad = gml[k] + carried(woutb, be_dst, k)
-        gml[k] = grad
-        return cross + grad * tile(k_li, k) * outm[k] * gain[pl.ds(k, 1), :]
-
-    cross = lax.fori_loop(0, nt, li_step, jnp.zeros((B, B), F32), unroll=True)
-    psum_start(cbuf, cross, c_s, c_r)
 
     gains = []
     for k in range(nt):

time: 44.8 us -> 42.8 us (0.955); the launches traced: 44.1 us -> 42.6 us
  Pallas kernels: 43.4 us -> 42 us
    pallas_call x1, Pallas kernels: 42.2 us -> 40.8 us  [on_device(): pl.pallas_call(functools.partial(kernel, n_seq, n_chan, nt), out_shape=[j...]
where the time goes in v5:
time: 42.8 us; the launch traced here: 42.6 us
  Pallas kernels  42 us (98%)
  between operations  0.64 us (1%)
    pallas_call x1, Pallas kernels, on_device(): pl.pallas_call(functools.partial(kernel, n_seq, n_chan, nt), out_shape=[j...  40.8 us
    pallas_call x1, Pallas kernels, on_device(): pl.pallas_call(deliver, out_shape=[jax.ShapeDtypeStruct(*shape) for shape...  1.21 us

profile of v5, /device:TPU:32, one launch (start us, length us, event | category | flops | bytes accessed | tf_op | source)
XLA Modules:
  0.0 42.6 jit_solution(7348602558538195003)
XLA Ops:
  0.6 40.8 %shard_map.161 = (bf16[128,1024]{1,0:T(8,128)(2,1)S(1)}, bf16[128,1024]{1,0:T(8,128)(2,1)S(1)}, bf16[128,1024]{1,0:T(8,128)(2,1)S(1)}, bf16[128,1024]{1,0:T(8,12...) custom-call(bf16[128,1024]{1,0:T(8,128)(2,1)} %q_mr_in.1, ...), custom_call_target="tpu_custom_call" | custom-call | tf_op jit(solution)/shard_map/pallas_call | solution.py:506
  41.4 1.2 %shard_map.162 = (bf16[128,1024]{1,0:T(8,128)(2,1)}, bf16[128,1024]{1,0:T(8,128)(2,1)}, bf16[128,1024]{1,0:T(8,128)(2,1)}, bf16[128,1024]{1,0:T(8,128)(2,1)}, bf...) custom-call(bf16[128,1024]{1,0:T(8,128)(2,1)S(1)} %get-tuple-element.24.refs_0_, ...), custom_call_target="tpu_custom_call" | custom-call | tf_op jit(solution)/shard_map/pallas_call | solution.py:529
